TPU v7x, 256 devices: a whole 4x4x8 slice. The times are simulated.
256 devices in a mesh: dp: 64 (over z, x_lo, y), mp: 4 (over x_hi, core).
Axes of the slice: x: 4 (x_hi: 2, x_lo: 2; x = x_hi * 2 + x_lo), y: 4, z: 8, core: 2. Of those that a mesh axis runs over, the one named last changes fastest.
Arguments:
- image_features: bfloat16 [10240, 1152], P('dp'), may hold values from -36 to 36
- text_features: bfloat16 [10240, 1152], P('dp'), may hold values from -36 to 36
- image_proj: bfloat16 [1152, 1152], P(None, 'mp'), may hold values from -0.75 to 0.75
- text_proj: bfloat16 [1152, 1152], P(None, 'mp'), may hold values from -0.75 to 0.75
- log_scale: float32 [1], replicated, may hold values from 4.3 to 4.7
- bias: float32 [1], replicated, may hold values from -11 to -9
Outputs:
- grad_image_features: float32 [10240, 1152], P('dp', 'mp')
- grad_text_features: float32 [10240, 1152], P('dp', 'mp')
- grad_image_proj: float32 [1152, 1152], P('dp', 'mp')
- grad_text_proj: float32 [1152, 1152], P('dp', 'mp')
All inputs are finite; a program needn't handle non-finite values.
Results may differ from a plain program's by a relative error of at most 0.0075.
Values may be sent and summed in bfloat16 or wider, within the bound.
No kernel may reach another device: no remote copies, remote signals or barrier semaphores. Data moves between devices by JAX's collectives and lax.ppermute only.
A program may use at most 128 MiB of HBM per device.

v0:
```python
import jax
import jax.numpy as jnp
from jax import lax
from jax.sharding import PartitionSpec as P


def normal_back(embedded, grads, inverse, inner):
    values = embedded.astype(jnp.float32)
    return (inverse * (grads - values * inner)).astype(jnp.bfloat16)


def shards(image_features, text_features, image_proj, text_proj, log_scale, bias):
    count = image_features.shape[0]
    position = lax.axis_index("dp")
    p_img = jnp.dot(image_features, image_proj, preferred_element_type=jnp.float32)
    p_txt = jnp.dot(text_features, text_proj, preferred_element_type=jnp.float32)
    sq_img, sq_txt = lax.psum(
        (
            jnp.sum(p_img * p_img, axis=1, keepdims=True),
            jnp.sum(p_txt * p_txt, axis=1, keepdims=True),
        ),
        "mp",
    )
    r_img = lax.rsqrt(sq_img + 1e-06)
    r_txt = lax.rsqrt(sq_txt + 1e-06)
    z_img = (p_img * r_img).astype(jnp.bfloat16)
    z_txt = (p_txt * r_txt).astype(jnp.bfloat16)
    width = z_img.shape[1]
    scale = jnp.exp(log_scale[0])
    offset = bias[0]
    texts = lax.all_gather(z_txt, "dp", axis=0, tiled=True)
    total_rows = texts.shape[0]
    span = 4 * count
    groups = total_rows // span
    row_base = position * count

    def derivative(partial_value, row_ids, col_ids):
        logits = scale * partial_value + offset
        sign = jnp.where(row_ids == col_ids, jnp.float32(1.0), jnp.float32(-1.0))
        return (-sign * jax.nn.sigmoid(-sign * logits) * scale).astype(jnp.bfloat16)

    def coefficients(partial_value, col_ids):
        total = lax.psum(partial_value, "mp")
        row_ids = row_base + jnp.arange(count, dtype=jnp.int32)[:, None]
        return derivative(total, row_ids, col_ids)

    store_start = jnp.zeros((total_rows, width), jnp.float32)

    def turn(group, carry):
        store, image_terms = carry
        start = (group * span).astype(jnp.int32)
        tile = lax.dynamic_slice_in_dim(texts, start, span, 0)
        partial_value = jnp.einsum("re,ce->rc", z_img, tile, preferred_element_type=jnp.float32)
        col_ids = start + jnp.arange(span, dtype=jnp.int32)[None, :]
        coef = coefficients(partial_value, col_ids)
        image_terms = image_terms + jnp.dot(coef, tile, preferred_element_type=jnp.float32)
        term = jnp.einsum("rc,re->ce", coef, z_img, preferred_element_type=jnp.float32)
        store = lax.dynamic_update_slice_in_dim(store, term, start, 0)
        return (store, image_terms)

    store, gz_img = lax.fori_loop(
        0, groups, turn, (store_start, jnp.zeros((count, width), jnp.float32))
    )
    gz_txt = lax.psum_scatter(store, "dp", scatter_dimension=0, tiled=True)
    inner_img, inner_txt = lax.psum(
        (
            jnp.sum(z_img.astype(jnp.float32) * gz_img, axis=1, keepdims=True),
            jnp.sum(z_txt.astype(jnp.float32) * gz_txt, axis=1, keepdims=True),
        ),
        "mp",
    )
    gp_img = normal_back(z_img, gz_img, r_img, inner_img)
    gp_txt = normal_back(z_txt, gz_txt, r_txt, inner_txt)
    feat_img = jnp.einsum("re,de->rd", gp_img, image_proj, preferred_element_type=jnp.float32)
    feat_txt = jnp.einsum("re,de->rd", gp_txt, text_proj, preferred_element_type=jnp.float32)
    grad_image_features, grad_text_features = (
        lax.psum_scatter(feat_img, "mp", scatter_dimension=1, tiled=True),
        lax.psum_scatter(feat_txt, "mp", scatter_dimension=1, tiled=True),
    )
    weight_img = jnp.einsum("rd,re->de", image_features, gp_img, preferred_element_type=jnp.float32)
    weight_txt = jnp.einsum("rd,re->de", text_features, gp_txt, preferred_element_type=jnp.float32)
    grad_image_proj, grad_text_proj = (
        lax.psum_scatter(weight_img, "dp", scatter_dimension=0, tiled=True),
        lax.psum_scatter(weight_txt, "dp", scatter_dimension=0, tiled=True),
    )
    return (grad_image_features, grad_text_features, grad_image_proj, grad_text_proj)


def solution(mesh):
    in_specs = (P("dp", None), P("dp", None), P(None, "mp"), P(None, "mp"), P(), P())
    out_specs = (P("dp", "mp"), P("dp", "mp"), P("dp", "mp"), P("dp", "mp"))
    return jax.shard_map(shards, mesh=mesh, in_specs=in_specs, out_specs=out_specs, check_vma=False)
```

profile of v0, /device:TPU:2, one launch (start us, length us, event | category | flops | bytes accessed | tf_op | source)
XLA Modules:
  0.0 2276.4 jit_solution(7794631599290595301)
XLA Ops:
  11.5 9.0 all-reduce.4
  22.2 308.6 %all-gather.2.cloned.1.call-done = bf16[10240,288]{1,0:T(8,128)(2,1)} async-done(((bf16[160,288]{1,0:T(8,128)(2,1)}), bf16[10240,288]{1,0:T(8,128)(2,1)}) %all-gather.2.cloned.1.call-update) | async-done | bytes 5898256 | tf_op jit(solution)/shard_map/all_gather | solution.py:31
  330.8 5.8 broadcast_in_dim.41
  336.5 878.4 %while.16 = (s32[]{:T(128)}, f32[10240,288]{0,1:T(8,128)}, f32[160,288]{1,0:T(8,128)S(1)}, s32[]{:T(128)}, f32[]{:T(128)}, /*index=5*/bf16[10240,288]{1,0:T(8,12...) while((s32[]{:T(128)}, f32[10240,288]{0,1:T(8,128)}, ...), condition=%wide.region_6.7_spmd.clone, body=%wide.region_4.6_spmd.clone.sunk | while | flops 179600160 | bytes 5971561 | solution.py:61
  338.8 49.2 %all-reduce.10.cloned.1.call-done = f32[160,640]{1,0:T(8,128)} async-done(((f32[160,640]{1,0:T(8,128)}), f32[160,640]{1,0:T(8,128)}) %all-reduce.10.cloned.1.call-update) | async-done | bytes 409616 | tf_op jit(solution)/shard_map/while/body/eval_jaxpr/psum | solution.py:43
  388.0 3.0 convolution_dynamic-update-slice_fusion.2
  395.6 47.4 %all-reduce.10.cloned.1.call-done = f32[160,640]{1,0:T(8,128)} async-done(((f32[160,640]{1,0:T(8,128)}), f32[160,640]{1,0:T(8,128)}) %all-reduce.10.cloned.1.call-update) | async-done | bytes 409616 | tf_op jit(solution)/shard_map/while/body/eval_jaxpr/psum | solution.py:43
  443.0 3.0 convolution_dynamic-update-slice_fusion.2
  450.5 47.1 %all-reduce.10.cloned.1.call-done = f32[160,640]{1,0:T(8,128)} async-done(((f32[160,640]{1,0:T(8,128)}), f32[160,640]{1,0:T(8,128)}) %all-reduce.10.cloned.1.call-update) | async-done | bytes 409616 | tf_op jit(solution)/shard_map/while/body/eval_jaxpr/psum | solution.py:43
  497.6 3.0 convolution_dynamic-update-slice_fusion.2
  505.2 47.1 %all-reduce.10.cloned.1.call-done = f32[160,640]{1,0:T(8,128)} async-done(((f32[160,640]{1,0:T(8,128)}), f32[160,640]{1,0:T(8,128)}) %all-reduce.10.cloned.1.call-update) | async-done | bytes 409616 | tf_op jit(solution)/shard_map/while/body/eval_jaxpr/psum | solution.py:43
  559.9 47.1 %all-reduce.10.cloned.1.call-done = f32[160,640]{1,0:T(8,128)} async-done(((f32[160,640]{1,0:T(8,128)}), f32[160,640]{1,0:T(8,128)}) %all-reduce.10.cloned.1.call-update) | async-done | bytes 409616 | tf_op jit(solution)/shard_map/while/body/eval_jaxpr/psum | solution.py:43
  607.0 3.1 convolution_dynamic-update-slice_fusion.2
  614.6 47.4 %all-reduce.10.cloned.1.call-done = f32[160,640]{1,0:T(8,128)} async-done(((f32[160,640]{1,0:T(8,128)}), f32[160,640]{1,0:T(8,128)}) %all-reduce.10.cloned.1.call-update) | async-done | bytes 409616 | tf_op jit(solution)/shard_map/while/body/eval_jaxpr/psum | solution.py:43
  669.5 47.4 %all-reduce.10.cloned.1.call-done = f32[160,640]{1,0:T(8,128)} async-done(((f32[160,640]{1,0:T(8,128)}), f32[160,640]{1,0:T(8,128)}) %all-reduce.10.cloned.1.call-update) | async-done | bytes 409616 | tf_op jit(solution)/shard_map/while/body/eval_jaxpr/psum | solution.py:43
  724.5 47.4 %all-reduce.10.cloned.1.call-done = f32[160,640]{1,0:T(8,128)} async-done(((f32[160,640]{1,0:T(8,128)}), f32[160,640]{1,0:T(8,128)}) %all-reduce.10.cloned.1.call-update) | async-done | bytes 409616 | tf_op jit(solution)/shard_map/while/body/eval_jaxpr/psum | solution.py:43
  779.4 47.1 %all-reduce.10.cloned.1.call-done = f32[160,640]{1,0:T(8,128)} async-done(((f32[160,640]{1,0:T(8,128)}), f32[160,640]{1,0:T(8,128)}) %all-reduce.10.cloned.1.call-update) | async-done | bytes 409616 | tf_op jit(solution)/shard_map/while/body/eval_jaxpr/psum | solution.py:43
  834.1 47.4 %all-reduce.10.cloned.1.call-done = f32[160,640]{1,0:T(8,128)} async-done(((f32[160,640]{1,0:T(8,128)}), f32[160,640]{1,0:T(8,128)}) %all-reduce.10.cloned.1.call-update) | async-done | bytes 409616 | tf_op jit(solution)/shard_map/while/body/eval_jaxpr/psum | solution.py:43
  889.0 47.1 %all-reduce.10.cloned.1.call-done = f32[160,640]{1,0:T(8,128)} async-done(((f32[160,640]{1,0:T(8,128)}), f32[160,640]{1,0:T(8,128)}) %all-reduce.10.cloned.1.call-update) | async-done | bytes 409616 | tf_op jit(solution)/shard_map/while/body/eval_jaxpr/psum | solution.py:43
  943.6 47.4 %all-reduce.10.cloned.1.call-done = f32[160,640]{1,0:T(8,128)} async-done(((f32[160,640]{1,0:T(8,128)}), f32[160,640]{1,0:T(8,128)}) %all-reduce.10.cloned.1.call-update) | async-done | bytes 409616 | tf_op jit(solution)/shard_map/while/body/eval_jaxpr/psum | solution.py:43
  998.6 47.1 %all-reduce.10.cloned.1.call-done = f32[160,640]{1,0:T(8,128)} async-done(((f32[160,640]{1,0:T(8,128)}), f32[160,640]{1,0:T(8,128)}) %all-reduce.10.cloned.1.call-update) | async-done | bytes 409616 | tf_op jit(solution)/shard_map/while/body/eval_jaxpr/psum | solution.py:43
  1045.7 3.0 convolution_dynamic-update-slice_fusion.2
  1053.3 47.1 %all-reduce.10.cloned.1.call-done = f32[160,640]{1,0:T(8,128)} async-done(((f32[160,640]{1,0:T(8,128)}), f32[160,640]{1,0:T(8,128)}) %all-reduce.10.cloned.1.call-update) | async-done | bytes 409616 | tf_op jit(solution)/shard_map/while/body/eval_jaxpr/psum | solution.py:43
  1107.9 47.1 %all-reduce.10.cloned.1.call-done = f32[160,640]{1,0:T(8,128)} async-done(((f32[160,640]{1,0:T(8,128)}), f32[160,640]{1,0:T(8,128)}) %all-reduce.10.cloned.1.call-update) | async-done | bytes 409616 | tf_op jit(solution)/shard_map/while/body/eval_jaxpr/psum | solution.py:43
  1155.0 3.0 convolution_dynamic-update-slice_fusion.2
  1162.6 47.1 %all-reduce.10.cloned.1.call-done = f32[160,640]{1,0:T(8,128)} async-done(((f32[160,640]{1,0:T(8,128)}), f32[160,640]{1,0:T(8,128)}) %all-reduce.10.cloned.1.call-update) | async-done | bytes 409616 | tf_op jit(solution)/shard_map/while/body/eval_jaxpr/psum | solution.py:43
  1215.0 14.3 copy.16
  1229.7 344.1 %reduce-scatter.10.cloned.1.call-done = f32[160,288]{1,0:T(8,128)} async-done(((f32[10240,288]{1,0:T(8,128)}), f32[160,288]{1,0:T(8,128)}) %reduce-scatter.10.cloned.1.call-update) | async-done | bytes 184336 | tf_op jit(solution)/shard_map/reduce_scatter | solution.py:64
  1574.9 7.2 all-reduce.3
  1590.7 34.5 %reduce-scatter.12.cloned.1.call-done = f32[288,160]{1,0:T(8,128)} async-done(((f32[1152,160]{1,0:T(8,128)}), f32[288,160]{1,0:T(8,128)}) %reduce-scatter.12.cloned.1.call-update) | async-done | bytes 184336
  1627.0 38.1 %reduce-scatter.14.cloned.1.call-done = f32[288,160]{1,0:T(8,128)} async-done(((f32[1152,160]{1,0:T(8,128)}), f32[288,160]{1,0:T(8,128)}) %reduce-scatter.14.cloned.1.call-update) | async-done | bytes 184336
  1666.9 599.1 %all-reduce.8.cloned.1.call-done = (f32[1152,288]{0,1:T(8,128)}, f32[1152,288]{0,1:T(8,128)}) async-done(((f32[1152,288]{0,1:T(8,128)}, f32[1152,288]{0,1:T(8,128)}), (f32[1152,288]{0,1:T(8,128)}, f32[1152,288]{0,1:T(8,128)})) %all-reduce.8.cloned.1.call-update) | async-done | bytes 2654224
  (147 shorter events, 123.3 us)
Async XLA Ops:
  7.2 1.1 copy-start
  7.2 323.6 %all-gather.2.cloned.1.call-start = ((), (), s32[]{:S(2)}) async-start(), calls=%async_computation.3 | async-start | bytes 7987200 | tf_op jit(solution)/shard_map/all_gather | solution.py:31
  336.5 51.5 %all-reduce.10.cloned.1.call-start = ((), (), s32[]{:S(2)}) async-start(), calls=%async_computation.8 | async-start | bytes 819200 | tf_op jit(solution)/shard_map/while/body/eval_jaxpr/psum | solution.py:43
  393.3 49.7 %all-reduce.10.cloned.1.call-start = ((), (), s32[]{:S(2)}) async-start(), calls=%async_computation.8 | async-start | bytes 819200 | tf_op jit(solution)/shard_map/while/body/eval_jaxpr/psum | solution.py:43
  448.3 49.4 %all-reduce.10.cloned.1.call-start = ((), (), s32[]{:S(2)}) async-start(), calls=%async_computation.8 | async-start | bytes 819200 | tf_op jit(solution)/shard_map/while/body/eval_jaxpr/psum | solution.py:43
  502.9 49.4 %all-reduce.10.cloned.1.call-start = ((), (), s32[]{:S(2)}) async-start(), calls=%async_computation.8 | async-start | bytes 819200 | tf_op jit(solution)/shard_map/while/body/eval_jaxpr/psum | solution.py:43
  557.6 49.4 %all-reduce.10.cloned.1.call-start = ((), (), s32[]{:S(2)}) async-start(), calls=%async_computation.8 | async-start | bytes 819200 | tf_op jit(solution)/shard_map/while/body/eval_jaxpr/psum | solution.py:43
  612.3 49.7 %all-reduce.10.cloned.1.call-start = ((), (), s32[]{:S(2)}) async-start(), calls=%async_computation.8 | async-start | bytes 819200 | tf_op jit(solution)/shard_map/while/body/eval_jaxpr/psum | solution.py:43
  667.2 49.7 %all-reduce.10.cloned.1.call-start = ((), (), s32[]{:S(2)}) async-start(), calls=%async_computation.8 | async-start | bytes 819200 | tf_op jit(solution)/shard_map/while/body/eval_jaxpr/psum | solution.py:43
  722.2 49.7 %all-reduce.10.cloned.1.call-start = ((), (), s32[]{:S(2)}) async-start(), calls=%async_computation.8 | async-start | bytes 819200 | tf_op jit(solution)/shard_map/while/body/eval_jaxpr/psum | solution.py:43
  777.1 49.4 %all-reduce.10.cloned.1.call-start = ((), (), s32[]{:S(2)}) async-start(), calls=%async_computation.8 | async-start | bytes 819200 | tf_op jit(solution)/shard_map/while/body/eval_jaxpr/psum | solution.py:43
  831.8 49.7 %all-reduce.10.cloned.1.call-start = ((), (), s32[]{:S(2)}) async-start(), calls=%async_computation.8 | async-start | bytes 819200 | tf_op jit(solution)/shard_map/while/body/eval_jaxpr/psum | solution.py:43
  886.7 49.4 %all-reduce.10.cloned.1.call-start = ((), (), s32[]{:S(2)}) async-start(), calls=%async_computation.8 | async-start | bytes 819200 | tf_op jit(solution)/shard_map/while/body/eval_jaxpr/psum | solution.py:43
  941.4 49.7 %all-reduce.10.cloned.1.call-start = ((), (), s32[]{:S(2)}) async-start(), calls=%async_computation.8 | async-start | bytes 819200 | tf_op jit(solution)/shard_map/while/body/eval_jaxpr/psum | solution.py:43
  996.3 49.4 %all-reduce.10.cloned.1.call-start = ((), (), s32[]{:S(2)}) async-start(), calls=%async_computation.8 | async-start | bytes 819200 | tf_op jit(solution)/shard_map/while/body/eval_jaxpr/psum | solution.py:43
  1051.0 49.4 %all-reduce.10.cloned.1.call-start = ((), (), s32[]{:S(2)}) async-start(), calls=%async_computation.8 | async-start | bytes 819200 | tf_op jit(solution)/shard_map/while/body/eval_jaxpr/psum | solution.py:43
  1105.6 49.4 %all-reduce.10.cloned.1.call-start = ((), (), s32[]{:S(2)}) async-start(), calls=%async_computation.8 | async-start | bytes 819200 | tf_op jit(solution)/shard_map/while/body/eval_jaxpr/psum | solution.py:43
  1160.3 49.4 %all-reduce.10.cloned.1.call-start = ((), (), s32[]{:S(2)}) async-start(), calls=%async_computation.8 | async-start | bytes 819200 | tf_op jit(solution)/shard_map/while/body/eval_jaxpr/psum | solution.py:43
  1215.0 358.8 %reduce-scatter.10.cloned.1.call-start = ((), (), s32[]{:S(2)}) async-start(), calls=%async_computation.4 | async-start | bytes 15974400 | tf_op jit(solution)/shard_map/reduce_scatter | solution.py:64
  1229.4 355.4 %copy-start.1 = (bf16[1152,288]{0,1:T(8,128)(2,1)S(1)}, bf16[1152,288]{0,1:T(8,128)(2,1)}, u32[]{:S(2)}) copy-start(bf16[1152,288]{0,1:T(8,128)(2,1)} %param.11) | copy-start | bytes 1990660
  1229.4 357.0 %copy-start.2 = (bf16[160,1152]{1,0:T(8,128)(2,1)S(1)}, bf16[160,1152]{1,0:T(8,128)(2,1)}, u32[]{:S(2)}) copy-start(bf16[160,1152]{1,0:T(8,128)(2,1)} %param.9) | copy-start | bytes 1105924
  1229.4 358.5 %copy-start.3 = (bf16[160,1152]{1,0:T(8,128)(2,1)S(1)}, bf16[160,1152]{1,0:T(8,128)(2,1)}, u32[]{:S(2)}) copy-start(bf16[160,1152]{1,0:T(8,128)(2,1)} %param.8) | copy-start | bytes 1105924
  1229.4 360.0 %copy-start.4 = (u32[256]{0:T(256)S(1)}, u32[256]{0:T(256)}, u32[]{:S(2)}) copy-start(u32[256]{0:T(256)} %constant.61) | copy-start | bytes 3076
  1229.4 395.7 %reduce-scatter.12.cloned.1.call-start = ((), (), s32[]{:S(2)}) async-start(), calls=%async_computation.5 | async-start | bytes 1474560
  1584.7 80.3 %reduce-scatter.14.cloned.1.call-start = ((), (), s32[]{:S(2)}) async-start(), calls=%async_computation.6 | async-start | bytes 1474560
  1586.4 679.6 %all-reduce.8.cloned.1.call-start = ((), (), s32[]{:S(2)}) async-start(), calls=%async_computation.7 | async-start | bytes 5308416
Sparse Core Ops, SparseCore 0:
  21.5 309.2 all-gather.1
  340.0 47.9 all-reduce.9
  396.8 46.1 all-reduce.9
  451.4 46.1 all-reduce.9
  506.1 46.1 all-reduce.9
  560.8 46.1 all-reduce.9
  615.8 46.1 all-reduce.9
  670.7 46.1 all-reduce.9
  725.7 46.1 all-reduce.9
  780.3 46.1 all-reduce.9
  835.3 46.1 all-reduce.9
  889.9 46.1 all-reduce.9
  944.9 46.1 all-reduce.9
  999.5 46.1 all-reduce.9
  1054.2 46.1 all-reduce.9
  1108.8 46.1 all-reduce.9
  1163.5 46.1 all-reduce.9
  1229.5 344.1 reduce-scatter.9
  1584.9 40.2 reduce-scatter.11
  1627.8 37.1 reduce-scatter.13
  1668.0 597.9 all-reduce.7
where the time goes:
time: 2280 us
  waiting for transfers between devices  2080 us (91%)
  matrix products  128 us (6%)
  local copies, waits for them, and re-layouts  28.9 us (1%)
    psum x16, waiting for transfers between devices, coefficients(): total = lax.psum(partial_value, 'mp')  758 us
    unnamed x8, waiting for transfers between devices  672 us
    reduce_scatter x1, waiting for transfers between devices, shards(): gz_txt = lax.psum_scatter(store, 'dp', scatter_dimension=0, tiled=True)  344 us
    all_gather x1, waiting for transfers between devices, shards(): texts = lax.all_gather(z_txt, 'dp', axis=0, tiled=True)  309 us
    dot_general x16, matrix products, turn(): jnp.einsum('rc,re->ce', coef, z_img, preferred_element_type=jnp.float32)  48.3 us
  transfers between devices with their start and end apart: 21, of which 21 were waited for; matrix products, arithmetic and copies ran while one was open for 0% of the time, Pallas kernels for 0%

commit v1 on v0

v1 whole, which is shorter than its diff:
```python
import jax
import jax.numpy as jnp
from jax import lax
from jax.sharding import Mesh, PartitionSpec as P

AXES = ("z", "xl", "y", "xh", "c")
SIZES = (8, 2, 4, 2, 2)
DP = ("z", "xl", "y")
MP = ("xh", "c")
PLANE = ("xl", "y", "xh")
BF = jnp.bfloat16
F32 = jnp.float32


def a2a(x, axes):
    return lax.all_to_all(x, axes, 0, 0, tiled=True)


def swap_core(x):
    return lax.ppermute(x, "c", [(0, 1), (1, 0)])


def rows_from_slices(pair):
    n = pair.shape[1] // 4
    parts = a2a(pair.reshape(2, 4, n, 288).transpose(1, 0, 2, 3), MP)
    return parts.transpose(1, 2, 0, 3).reshape(2, n, 1152)


def slices_from_rows(pair):
    n = pair.shape[1]
    parts = a2a(pair.reshape(2, n, 4, 288).transpose(2, 0, 1, 3), MP)
    return parts.transpose(1, 0, 2, 3).reshape(2, 4 * n, 288)


def shards(image_features, text_features, image_proj, text_proj, log_scale, bias):
    zi = lax.axis_index("z")
    ci = lax.axis_index("c")
    xl, y, xh = lax.axis_index("xl"), lax.axis_index("y"), lax.axis_index("xh")
    p_img = jnp.dot(image_features, image_proj, preferred_element_type=F32)
    p_txt = jnp.dot(text_features, text_proj, preferred_element_type=F32)
    own = rows_from_slices(jnp.stack([p_img, p_txt]).astype(BF)).astype(F32)
    r = lax.rsqrt(jnp.sum(own * own, axis=2, keepdims=True) + 1e-06)
    z = (own * r).astype(BF)
    z_img, z_txt = z[0], z[1]
    r_img, r_txt = r[0], r[1]

    txt_own = a2a(jnp.broadcast_to(z_txt[None], (8, 40, 1152)), ("z",)).reshape(320, 1152)
    img = a2a(jnp.broadcast_to(z_img[None], (16, 40, 1152)), PLANE).reshape(640, 1152)
    txt_oth = swap_core(txt_own)

    scale = jnp.exp(log_scale[0])
    offset = bias[0]
    place = (xl * 4 + y) * 2 + xh
    row_ids = jnp.arange(640, dtype=jnp.int32)[:, None] - place * 40
    col_ids = jnp.arange(320, dtype=jnp.int32)[None, :] - zi * 40
    diag = (row_ids == col_ids) & (row_ids >= 0) & (row_ids < 40)

    def coefs(txt, mask):
        d = jnp.einsum("re,ce->rc", img, txt, preferred_element_type=F32)
        logits = scale * d + offset
        if mask is None:
            return (scale * jax.nn.sigmoid(logits)).astype(BF)
        sign = jnp.where(mask, F32(1.0), F32(-1.0))
        return (-sign * jax.nn.sigmoid(-sign * logits) * scale).astype(BF)

    coef_oth = coefs(txt_oth, None)
    coef_own = coefs(txt_own, diag)
    t_oth = jnp.einsum("rc,re->ce", coef_oth, img, preferred_element_type=F32).astype(BF)
    t_got = swap_core(t_oth)
    t_own = jnp.einsum("rc,re->ce", coef_own, img, preferred_element_type=F32)
    t_sum = (t_own + t_got.astype(F32)).astype(BF).reshape(8, 40, 1152)
    g_img = (
        jnp.dot(coef_own, txt_own, preferred_element_type=F32)
        + jnp.dot(coef_oth, txt_oth, preferred_element_type=F32)
    ).astype(BF).reshape(16, 40, 1152)
    gz_txt = jnp.sum(a2a(t_sum, ("z",)).astype(F32), axis=0)
    gz_img = jnp.sum(a2a(g_img, PLANE).astype(F32), axis=0)

    gz = jnp.stack([gz_img, gz_txt])
    values = z.astype(F32)
    inner = jnp.sum(values * gz, axis=2, keepdims=True)
    gp_rows = (r * (gz - values * inner)).astype(BF)
    gp = slices_from_rows(gp_rows)
    gp_img, gp_txt = gp[0], gp[1]

    w_img = jnp.einsum("rd,re->de", image_features, gp_img, preferred_element_type=F32)
    w_txt = jnp.einsum("rd,re->de", text_features, gp_txt, preferred_element_type=F32)
    w = jnp.stack([w_img, w_txt]).astype(BF).reshape(2, 8, 8, 18, 288)
    w = w.transpose(2, 0, 1, 3, 4).reshape(8, 2 * 144, 288)
    w = jnp.sum(a2a(w, ("xl", "y")).astype(F32), axis=0).astype(BF)
    w = w.reshape(2, 8, 18, 288).transpose(1, 0, 2, 3)
    w = jnp.sum(a2a(w, ("z",)).astype(F32), axis=0)

    f_img = jnp.einsum("re,de->rd", gp_img, image_proj, preferred_element_type=F32)
    f_txt = jnp.einsum("re,de->rd", gp_txt, text_proj, preferred_element_type=F32)
    f = jnp.stack([f_img, f_txt]).astype(BF).reshape(2, 160, 4, 288).transpose(2, 0, 1, 3)
    f = jnp.sum(a2a(f, MP).astype(F32), axis=0)
    return f[0], f[1], w[0], w[1]


def solution(mesh):
    fine = Mesh(mesh.devices.reshape(SIZES), AXES)
    in_specs = (P(DP, None), P(DP, None), P(None, MP), P(None, MP), P(), P())
    out_specs = (P(DP, MP), P(DP, MP), P(DP, MP), P(DP, MP))
    return jax.shard_map(shards, mesh=fine, in_specs=in_specs, out_specs=out_specs, check_vma=False)
```

time: 2280 us -> 214 us (0.09)
  waiting for transfers between devices: 2080 us -> 93.4 us
  matrix products: 128 us -> 17.4 us
  blocking collectives: 16.2 us -> 50.9 us
  starting transfers between devices: 0.85 us -> 30.2 us
    psum x16 -> x0, waiting for transfers between devices: 758 us -> none  [coefficients(): total = lax.psum(partial_value, 'mp')]
    unnamed x8 -> x0, waiting for transfers between devices: 672 us -> none
    reduce_scatter x1 -> x0, waiting for transfers between devices: 344 us -> none  [shards(): gz_txt = lax.psum_scatter(store, 'dp', scatter_dimension=0, tiled=True)]
    all_gather x1 -> x0, waiting for transfers between devices: 309 us -> none  [shards(): texts = lax.all_gather(z_txt, 'dp', axis=0, tiled=True)]
    dot_general x52 -> x12, matrix products: 125 us -> 17.4 us  [the longest x1 3.45 us: shards(): jnp.dot(coef_oth, txt_oth, preferred_element_type=F32)]
    all_to_all x0 -> x6, waiting for transfers between devices: none -> 91.2 us  [a2a(): return lax.all_to_all(x, axes, 0, 0, tiled=True)]
    all_to_all x0 -> x3, blocking collectives: none -> 50.9 us  [a2a(): return lax.all_to_all(x, axes, 0, 0, tiled=True)]
    all_to_all x0 -> x6, starting transfers between devices: none -> 30 us  [a2a(): return lax.all_to_all(x, axes, 0, 0, tiled=True)]
  transfers between devices with their start and end apart: 21 -> 8, of which waited for: 21 -> 7; matrix products, arithmetic and copies ran while one was open for 0% -> 7% of each run, Pallas kernels for 0% -> 0%
where the time goes in v1:
time: 214 us; the launch traced here: 213 us
  waiting for transfers between devices  93.4 us (44%)
  blocking collectives  50.9 us (24%)
  starting transfers between devices  30.2 us (14%)
  matrix products  17.4 us (8%)
  local copies, waits for them, and re-layouts  15.4 us (7%)
  other arithmetic  3.81 us (2%)
  between operations  2.31 us (1%)
    all_to_all x6, waiting for transfers between devices, a2a(): return lax.all_to_all(x, axes, 0, 0, tiled=True)  91.2 us
    all_to_all x3, blocking collectives, a2a(): return lax.all_to_all(x, axes, 0, 0, tiled=True)  50.9 us
    all_to_all x6, starting transfers between devices, a2a(): return lax.all_to_all(x, axes, 0, 0, tiled=True)  30 us
  transfers between devices with their start and end apart: 8, of which 7 were waited for; matrix products, arithmetic and copies ran while one was open for 7% of the time, Pallas kernels for 0%

profile of v1, /device:TPU:2, one launch (start us, length us, event | category | flops | bytes accessed | tf_op | source)
XLA Modules:
  0.0 213.4 jit_solution(16883518924499918919)
XLA Ops:
  1.6 1.5 convolution_convert_fusion.6
  3.1 1.6 convolution_convert_fusion.5
  4.8 10.6 %all_to_all.45 = bf16[4,2,40,288]{3,2,1,0:T(8,128)(2,1)S(1)} all-to-all(bf16[4,2,40,288]{3,2,1,0:T(8,128)(2,1)S(1)} %maximum_bitcast_fusion.2), channel_id=1, replica_groups=mesh['z'=8,'xl'=2,'y'=4,'xh'=2,'c'=2] {'xh','c'}, dimensions={0} | all-to-all | bytes 368640 | tf_op jit(solution)/shard_map/all_to_all | solution.py:16
  16.3 30.0 %all_to_all.46 = bf16[8,40,1152]{2,1,0:T(8,128)(2,1)S(1)} all-to-all(bf16[8,40,1152]{2,1,0:T(8,128)(2,1)S(1)} %broadcast_in_dim.31), channel_id=1, replica_groups=mesh['z'=8,'xl'=2,'y'=4,'xh'=2,'c'=2] {'z'}, dimensions={0} | all-to-all | bytes 1474560 | tf_op jit(solution)/shard_map/all_to_all | solution.py:16
  46.3 1.2 broadcast_in_dim.29
  47.6 6.1 %all-to-all-start.1 = ((bf16[16,40,1152]{2,1,0:T(8,128)(2,1)}), bf16[16,40,1152]{2,1,0:T(8,128)(2,1)S(1)}, u32[]{:S(2)}, u32[]{:S(2)}) async-start(bf16[16,40,1152]{2,1,0:T(8,128)(2,1)} %broadcast_in_dim.29), calls=%async_computation.1 | async-start | bytes 2949120 | tf_op jit(solution)/shard_map/all_to_all | solution.py:16
  55.2 16.9 %all-to-all-done.1 = bf16[16,40,1152]{2,1,0:T(8,128)(2,1)S(1)} async-done(((bf16[16,40,1152]{2,1,0:T(8,128)(2,1)}), bf16[16,40,1152]{2,1,0:T(8,128)(2,1)S(1)}, u32[]{:S(2)}, u32[]{:S(2)}) %all-to-all-start.1) | async-done | bytes 1474592 | tf_op jit(solution)/shard_map/all_to_all | solution.py:16
  73.0 1.0 fusion.32
  74.1 2.0 fusion.17
  76.1 3.4 %fusion = bf16[640,1152]{1,0:T(8,128)(2,1)} fusion(f32[640,1152]{1,0:T(8,128)S(1)} %fusion.32, bf16[640,320]{0,1:T(8,128)(2,1)S(1)} %fusion.17, bf16[320,1152]{1,0:T(8,128)(2,1)} %collective-permute-done), kind=kOutput, calls=%fused_computation.1 | convolution fusion | flops 473333760 | bytes 5570560 | tf_op jit(solution)/shard_map/dot_general | solution.py:74
  79.5 6.3 %all-to-all-start.3 = ((bf16[16,40,1152]{2,1,0:T(8,128)(2,1)}), bf16[16,40,1152]{2,1,0:T(8,128)(2,1)S(1)}, u32[]{:S(2)}, u32[]{:S(2)}) async-start(bf16[16,40,1152]{2,1,0:T(8,128)(2,1)} %bitcast.95), calls=%async_computation.3 | async-start | bytes 2949120 | tf_op jit(solution)/shard_map/all_to_all | solution.py:16
  85.9 2.3 %convolution_convert_fusion = bf16[320,1152]{1,0:T(8,128)(2,1)S(1)} fusion(bf16[640,320]{0,1:T(8,128)(2,1)S(1)} %copy-done.6, bf16[640,1152]{1,0:T(8,128)(2,1)} %bitcast.103), kind=kOutput, calls=%fused_computation.3 | convolution fusion | flops 472227840 | bytes 2621440 | tf_op jit(solution)/shard_map/rc,re->ce/dot_general | solution.py:68
  88.2 2.2 %collective-permute-done.1 = bf16[320,1152]{1,0:T(8,128)(2,1)S(1)} collective-permute-done((bf16[320,1152]{1,0:T(8,128)(2,1)S(1)}, bf16[320,1152]{1,0:T(8,128)(2,1)S(1)}, u32[]{:S(2)}, u32[]{:S(2)}) %collective-permute-start.1) | collective-permute-done | bytes 737312 | tf_op jit(solution)/shard_map/ppermute | solution.py:20
  90.4 1.7 add_convert_fusion
  92.1 12.7 %all-to-all-done.3 = bf16[16,40,1152]{2,1,0:T(8,128)(2,1)S(1)} async-done(((bf16[16,40,1152]{2,1,0:T(8,128)(2,1)}), bf16[16,40,1152]{2,1,0:T(8,128)(2,1)S(1)}, u32[]{:S(2)}, u32[]{:S(2)}) %all-to-all-start.3) | async-done | bytes 1474592 | tf_op jit(solution)/shard_map/all_to_all | solution.py:16
  104.8 5.5 %all-to-all-start.4 = ((bf16[8,40,1152]{2,1,0:T(8,128)(2,1)}), bf16[8,40,1152]{2,1,0:T(8,128)(2,1)S(1)}, u32[]{:S(2)}, u32[]{:S(2)}) async-start(bf16[8,40,1152]{2,1,0:T(8,128)(2,1)} %bitcast.111), calls=%async_computation.4 | async-start | bytes 1474560 | tf_op jit(solution)/shard_map/all_to_all | solution.py:16
  110.8 21.8 %all-to-all-done.4 = bf16[8,40,1152]{2,1,0:T(8,128)(2,1)S(1)} async-done(((bf16[8,40,1152]{2,1,0:T(8,128)(2,1)}), bf16[8,40,1152]{2,1,0:T(8,128)(2,1)S(1)}, u32[]{:S(2)}, u32[]{:S(2)}) %all-to-all-start.4) | async-done | bytes 737312 | tf_op jit(solution)/shard_map/all_to_all | solution.py:16
  132.9 1.1 fusion.23
  134.4 10.4 %all_to_all.47 = bf16[4,2,40,288]{3,2,1,0:T(8,128)(2,1)S(1)} all-to-all(bf16[4,2,40,288]{3,2,1,0:T(8,128)(2,1)S(1)} %copy.36), channel_id=1, replica_groups=mesh['z'=8,'xl'=2,'y'=4,'xh'=2,'c'=2] {'xh','c'}, dimensions={0} | all-to-all | bytes 368640 | tf_op jit(solution)/shard_map/all_to_all | solution.py:16
  146.6 1.2 copy.41
  147.8 1.6 stack.40
  150.2 1.5 copy.43
  151.7 5.1 %all-to-all-start.7 = ((bf16[8,288,288]{2,1,0:T(8,128)(2,1)}), bf16[8,288,288]{2,1,0:T(8,128)(2,1)S(1)}, u32[]{:S(2)}, u32[]{:S(2)}) async-start(bf16[8,288,288]{2,1,0:T(8,128)(2,1)} %copy.43), calls=%async_computation.7 | async-start | bytes 3538944 | tf_op jit(solution)/shard_map/all_to_all | solution.py:16
  156.8 1.2 copy.45
  158.0 1.5 copy.46
  159.5 1.7 fusion.19
  161.9 1.1 copy.39
  162.9 15.8 %all-to-all-done.7 = bf16[8,288,288]{2,1,0:T(8,128)(2,1)S(1)} async-done(((bf16[8,288,288]{2,1,0:T(8,128)(2,1)}), bf16[8,288,288]{2,1,0:T(8,128)(2,1)S(1)}, u32[]{:S(2)}, u32[]{:S(2)}) %all-to-all-start.7) | async-done | bytes 1327136 | tf_op jit(solution)/shard_map/all_to_all | solution.py:16
  178.7 3.5 %all-to-all-start.6 = ((bf16[4,2,160,288]{3,2,1,0:T(8,128)(2,1)}), bf16[4,2,160,288]{3,2,1,0:T(8,128)(2,1)S(1)}, u32[]{:S(2)}, u32[]{:S(2)}) async-start(bf16[4,2,160,288]{3,2,1,0:T(8,128)(2,1)} %copy.39), calls=%async_computation.6 | async-start | bytes 1966080 | tf_op jit(solution)/shard_map/all_to_all | solution.py:16
  183.6 13.9 %all-to-all-done.6 = bf16[4,2,160,288]{3,2,1,0:T(8,128)(2,1)S(1)} async-done(((bf16[4,2,160,288]{3,2,1,0:T(8,128)(2,1)}), bf16[4,2,160,288]{3,2,1,0:T(8,128)(2,1)S(1)}, u32[]{:S(2)}, u32[]{:S(2)}) %all-to-all-start.6) | async-done | bytes 737312 | tf_op jit(solution)/shard_map/all_to_all | solution.py:16
  197.5 3.4 %all-to-all-start.8 = ((bf16[8,2,18,288]{3,1,2,0:T(2,128)(2,1)}), bf16[8,2,18,288]{3,1,2,0:T(2,128)(2,1)S(1)}, u32[]{:S(2)}, u32[]{:S(2)}) async-start(bf16[8,2,18,288]{3,1,2,0:T(2,128)(2,1)} %copy.44), calls=%async_computation.8 | async-start | bytes 442368 | tf_op jit(solution)/shard_map/all_to_all | solution.py:16
  201.9 10.0 %all-to-all-done.8 = bf16[8,2,18,288]{3,1,2,0:T(2,128)(2,1)S(1)} async-done(((bf16[8,2,18,288]{3,1,2,0:T(2,128)(2,1)}), bf16[8,2,18,288]{3,1,2,0:T(2,128)(2,1)S(1)}, u32[]{:S(2)}, u32[]{:S(2)}) %all-to-all-start.8) | async-done | bytes 165920 | tf_op jit(solution)/shard_map/all_to_all | solution.py:16
  (55 shorter events, 11.2 us)
Async XLA Ops:
  0.6 1.0 copy-start
  47.6 24.5 %all-to-all-start.1 = ((bf16[16,40,1152]{2,1,0:T(8,128)(2,1)}), bf16[16,40,1152]{2,1,0:T(8,128)(2,1)S(1)}, u32[]{:S(2)}, u32[]{:S(2)}) async-start(bf16[16,40,1152]{2,1,0:T(8,128)(2,1)} %broadcast_in_dim.29), calls=%async_computation.1 | async-start | bytes 2949120 | tf_op jit(solution)/shard_map/all_to_all | solution.py:16
  53.7 20.3 %collective-permute-start = (bf16[320,1152]{1,0:T(8,128)(2,1)S(1)}, bf16[320,1152]{1,0:T(8,128)(2,1)}, u32[]{:S(2)}, u32[]{:S(2)}) collective-permute-start(bf16[320,1152]{1,0:T(8,128)(2,1)S(1)} %bitcast.98), channel_id=1, source_target_pairs={{0,1},{1,0},{2,3},{3,2},{4,5},{5,4},{6,7},{7,6},{8,9},{9,8},{10,11... | collective-permute-start | bytes 2211848 | tf_op jit(solution)/shard_map/ppermute | solution.py:20
  72.1 2.0 copy-start.2
  76.1 3.5 %copy-start.5 = (bf16[640,320]{0,1:T(8,128)(2,1)}, bf16[640,320]{0,1:T(8,128)(2,1)S(1)}, u32[]{:S(2)}) copy-start(bf16[640,320]{0,1:T(8,128)(2,1)S(1)} %fusion.17) | copy-start | bytes 1228804
  79.5 6.3 %copy-start.6 = (bf16[640,320]{0,1:T(8,128)(2,1)S(1)}, bf16[640,320]{0,1:T(8,128)(2,1)}, u32[]{:S(2)}) copy-start(bf16[640,320]{0,1:T(8,128)(2,1)} %copy-done.5) | copy-start | bytes 1228804
  79.5 25.3 %all-to-all-start.3 = ((bf16[16,40,1152]{2,1,0:T(8,128)(2,1)}), bf16[16,40,1152]{2,1,0:T(8,128)(2,1)S(1)}, u32[]{:S(2)}, u32[]{:S(2)}) async-start(bf16[16,40,1152]{2,1,0:T(8,128)(2,1)} %bitcast.95), calls=%async_computation.3 | async-start | bytes 2949120 | tf_op jit(solution)/shard_map/all_to_all | solution.py:16
  85.8 4.6 %copy-start.3 = (bf16[16,40,1152]{2,1,0:T(8,128)(2,1)S(1)}, bf16[16,40,1152]{2,1,0:T(8,128)(2,1)}, u32[]{:S(2)}) copy-start(bf16[16,40,1152]{2,1,0:T(8,128)(2,1)} %copy-done.2) | copy-start | bytes 4423684
  88.1 2.3 %collective-permute-start.1 = (bf16[320,1152]{1,0:T(8,128)(2,1)S(1)}, bf16[320,1152]{1,0:T(8,128)(2,1)S(1)}, u32[]{:S(2)}, u32[]{:S(2)}) collective-permute-start(bf16[320,1152]{1,0:T(8,128)(2,1)S(1)} %convolution_convert_fusion), channel_id=1, source_target_pairs={{0,1},{1,0},{2,3},{3,2},{4,5},{5,4},{6,7},{7,6},{8,9},{9,8},{10,11... | collective-permute-start | bytes 2211848 | tf_op jit(solution)/shard_map/ppermute | solution.py:20
  104.8 27.7 %all-to-all-start.4 = ((bf16[8,40,1152]{2,1,0:T(8,128)(2,1)}), bf16[8,40,1152]{2,1,0:T(8,128)(2,1)S(1)}, u32[]{:S(2)}, u32[]{:S(2)}) async-start(bf16[8,40,1152]{2,1,0:T(8,128)(2,1)} %bitcast.111), calls=%async_computation.4 | async-start | bytes 1474560 | tf_op jit(solution)/shard_map/all_to_all | solution.py:16
  145.2 1.0 copy-start.4
  151.7 5.1 %copy-start.1 = (bf16[1152,288]{0,1:T(8,128)(2,1)S(1)}, bf16[1152,288]{0,1:T(8,128)(2,1)}, u32[]{:S(2)}) copy-start(bf16[1152,288]{0,1:T(8,128)(2,1)} %param.8) | copy-start | bytes 1990660
  151.7 27.1 %all-to-all-start.7 = ((bf16[8,288,288]{2,1,0:T(8,128)(2,1)}), bf16[8,288,288]{2,1,0:T(8,128)(2,1)S(1)}, u32[]{:S(2)}, u32[]{:S(2)}) async-start(bf16[8,288,288]{2,1,0:T(8,128)(2,1)} %copy.43), calls=%async_computation.7 | async-start | bytes 3538944 | tf_op jit(solution)/shard_map/all_to_all | solution.py:16
  178.7 18.7 %all-to-all-start.6 = ((bf16[4,2,160,288]{3,2,1,0:T(8,128)(2,1)}), bf16[4,2,160,288]{3,2,1,0:T(8,128)(2,1)S(1)}, u32[]{:S(2)}, u32[]{:S(2)}) async-start(bf16[4,2,160,288]{3,2,1,0:T(8,128)(2,1)} %copy.39), calls=%async_computation.6 | async-start | bytes 1966080 | tf_op jit(solution)/shard_map/all_to_all | solution.py:16
  197.5 14.4 %all-to-all-start.8 = ((bf16[8,2,18,288]{3,1,2,0:T(2,128)(2,1)}), bf16[8,2,18,288]{3,1,2,0:T(2,128)(2,1)S(1)}, u32[]{:S(2)}, u32[]{:S(2)}) async-start(bf16[8,2,18,288]{3,1,2,0:T(2,128)(2,1)} %copy.44), calls=%async_computation.8 | async-start | bytes 442368 | tf_op jit(solution)/shard_map/all_to_all | solution.py:16

commit v2 on v1

--- a/solution.py
+++ b/solution.py
@@ -20,6 +20,15 @@
     return lax.ppermute(x, "c", [(0, 1), (1, 0)])
 
 
+def shift(x, axis, size, step):
+    return lax.ppermute(x, axis, [(i, (i + step) % size) for i in range(size)])
+
+
+def mp_shift(x, dx, dc):
+    pairs = [(a * 2 + b, (a ^ dx) * 2 + (b ^ dc)) for a in range(2) for b in range(2)]
+    return lax.ppermute(x, MP, pairs)
+
+
 def rows_from_slices(pair):
     n = pair.shape[1] // 4
     parts = a2a(pair.reshape(2, 4, n, 288).transpose(1, 0, 2, 3), MP)
@@ -33,26 +42,24 @@
 
 
 def shards(image_features, text_features, image_proj, text_proj, log_scale, bias):
-    zi = lax.axis_index("z")
-    ci = lax.axis_index("c")
-    xl, y, xh = lax.axis_index("xl"), lax.axis_index("y"), lax.axis_index("xh")
+    xl, y, xh, c = (lax.axis_index(a) for a in AXES[1:])
     p_img = jnp.dot(image_features, image_proj, preferred_element_type=F32)
     p_txt = jnp.dot(text_features, text_proj, preferred_element_type=F32)
-    own = rows_from_slices(jnp.stack([p_img, p_txt]).astype(BF)).astype(F32)
+    own = rows_from_slices(jnp.stack([p_img, p_txt]))
     r = lax.rsqrt(jnp.sum(own * own, axis=2, keepdims=True) + 1e-06)
     z = (own * r).astype(BF)
     z_img, z_txt = z[0], z[1]
     r_img, r_txt = r[0], r[1]
 
-    txt_own = a2a(jnp.broadcast_to(z_txt[None], (8, 40, 1152)), ("z",)).reshape(320, 1152)
     img = a2a(jnp.broadcast_to(z_img[None], (16, 40, 1152)), PLANE).reshape(640, 1152)
+    txt_own = jnp.concatenate([z_txt] + [shift(z_txt, "z", 8, d) for d in range(1, 8)])
     txt_oth = swap_core(txt_own)
 
     scale = jnp.exp(log_scale[0])
     offset = bias[0]
     place = (xl * 4 + y) * 2 + xh
     row_ids = jnp.arange(640, dtype=jnp.int32)[:, None] - place * 40
-    col_ids = jnp.arange(320, dtype=jnp.int32)[None, :] - zi * 40
+    col_ids = jnp.arange(320, dtype=jnp.int32)[None, :]
     diag = (row_ids == col_ids) & (row_ids >= 0) & (row_ids < 40)
 
     def coefs(txt, mask):
@@ -68,12 +75,15 @@
     t_oth = jnp.einsum("rc,re->ce", coef_oth, img, preferred_element_type=F32).astype(BF)
     t_got = swap_core(t_oth)
     t_own = jnp.einsum("rc,re->ce", coef_own, img, preferred_element_type=F32)
-    t_sum = (t_own + t_got.astype(F32)).astype(BF).reshape(8, 40, 1152)
+    t_sum = t_own + t_got.astype(F32)
+    t_out = t_sum[40:].astype(BF)
+    gz_txt = t_sum[:40]
+    for d in range(1, 8):
+        gz_txt = gz_txt + shift(t_out[40 * d - 40 : 40 * d], "z", 8, -d).astype(F32)
     g_img = (
         jnp.dot(coef_own, txt_own, preferred_element_type=F32)
         + jnp.dot(coef_oth, txt_oth, preferred_element_type=F32)
     ).astype(BF).reshape(16, 40, 1152)
-    gz_txt = jnp.sum(a2a(t_sum, ("z",)).astype(F32), axis=0)
     gz_img = jnp.sum(a2a(g_img, PLANE).astype(F32), axis=0)
 
     gz = jnp.stack([gz_img, gz_txt])
@@ -93,8 +103,14 @@
 
     f_img = jnp.einsum("re,de->rd", gp_img, image_proj, preferred_element_type=F32)
     f_txt = jnp.einsum("re,de->rd", gp_txt, text_proj, preferred_element_type=F32)
-    f = jnp.stack([f_img, f_txt]).astype(BF).reshape(2, 160, 4, 288).transpose(2, 0, 1, 3)
-    f = jnp.sum(a2a(f, MP).astype(F32), axis=0)
+    f = jnp.stack([f_img, f_txt]).reshape(2, 160, 4, 288).transpose(2, 0, 1, 3)
+    me = xh * 2 + c
+    total = lax.dynamic_index_in_dim(f, me, 0, keepdims=False)
+    f = f.astype(BF)
+    for dx, dc in ((0, 1), (1, 0), (1, 1)):
+        other = lax.dynamic_index_in_dim(f, (xh ^ dx) * 2 + (c ^ dc), 0, keepdims=False)
+        total = total + mp_shift(other, dx, dc).astype(F32)
+    f = total
     return f[0], f[1], w[0], w[1]
 
 

time: 214 us -> 170 us (0.79)
  waiting for transfers between devices: 93.4 us -> 39.5 us
  starting transfers between devices: 30.2 us -> 60.9 us
  blocking collectives: 50.9 us -> 23.7 us
  local copies, waits for them, and re-layouts: 15.4 us -> 20.5 us
  other arithmetic: 3.81 us -> 7.68 us
  matrix products: 17.4 us -> 14.6 us
    all_to_all x6 -> x4, waiting for transfers between devices: 91.2 us -> 29.4 us  [a2a(): return lax.all_to_all(x, axes, 0, 0, tiled=True)]
    ppermute x0 -> x17, starting transfers between devices: none -> 38.9 us  [the longest x14 35.5 us: shift(): return lax.ppermute(x, axis, [(i, (i + step) % size) for i in range(size)])]
    all_to_all x3 -> x2, blocking collectives: 50.9 us -> 23.7 us  [a2a(): return lax.all_to_all(x, axes, 0, 0, tiled=True)]
    ppermute x0 -> x17, waiting for transfers between devices: none -> 8.91 us  [the longest x14 8.51 us: shift(): return lax.ppermute(x, axis, [(i, (i + step) % size) for i in range(size)])]
    all_to_all x6 -> x4, starting transfers between devices: 30 us -> 22 us  [a2a(): return lax.all_to_all(x, axes, 0, 0, tiled=True)]
    unnamed x17 -> x24, local copies, waits for them, and re-layouts: 2.5 us -> 8.09 us
  transfers between devices with their start and end apart: 8 -> 23, of which waited for: 7 -> 9; matrix products, arithmetic and copies ran while one was open for 7% -> 13% of each run, Pallas kernels for 0% -> 0%
where the time goes in v2:
time: 170 us; the launch traced here: 169 us
  starting transfers between devices  60.9 us (36%)
  waiting for transfers between devices  39.5 us (23%)
  blocking collectives  23.7 us (14%)
  local copies, waits for them, and re-layouts  20.5 us (12%)
  matrix products  14.6 us (9%)
  other arithmetic  7.68 us (5%)
  between operations  2.32 us (1%)
    ppermute x14, starting transfers between devices, shift(): return lax.ppermute(x, axis, [(i, (i + step) % size) for i in range(size)])  35.5 us
    all_to_all x4, waiting for transfers between devices, a2a(): return lax.all_to_all(x, axes, 0, 0, tiled=True)  29.4 us
    all_to_all x2, blocking collectives, a2a(): return lax.all_to_all(x, axes, 0, 0, tiled=True)  23.7 us
    all_to_all x4, starting transfers between devices, a2a(): return lax.all_to_all(x, axes, 0, 0, tiled=True)  22 us
    ppermute x14, waiting for transfers between devices, shift(): return lax.ppermute(x, axis, [(i, (i + step) % size) for i in range(size)])  8.51 us
    unnamed x24, local copies, waits for them, and re-layouts  8.09 us
  transfers between devices with their start and end apart: 23, of which 9 were waited for; matrix products, arithmetic and copies ran while one was open for 13% of the time, Pallas kernels for 0%

profile of v2, /device:TPU:2, one launch (start us, length us, event | category | flops | bytes accessed | tf_op | source)
XLA Modules:
  0.0 169.2 jit_solution(654900757933115903)
XLA Ops:
  1.6 1.5 fusion.44
  3.6 13.2 %all_to_all.30 = f32[4,2,40,288]{3,2,1,0:T(8,128)S(1)} all-to-all(f32[4,2,40,288]{3,2,1,0:T(8,128)S(1)} %maximum_bitcast_fusion.1), channel_id=1, replica_groups=mesh['z'=8,'xl'=2,'y'=4,'xh'=2,'c'=2] {'xh','c'}, dimensions={0} | all-to-all | bytes 737280 | tf_op jit(solution)/shard_map/all_to_all | solution.py:16
  17.8 2.0 %collective-permute-start = (bf16[40,1152]{1,0:T(8,128)(2,1)S(1)}, bf16[40,1152]{1,0:T(8,128)(2,1)S(1)}, u32[]{:S(2)}, u32[]{:S(2)}) collective-permute-start(bf16[40,1152]{1,0:T(8,128)(2,1)S(1)} %get-tuple-element.20), channel_id=1, source_target_pairs={{0,32},{32,64},{64,96},{96,128},{128,160},{160,192},{192,224},{224... | collective-permute-start | bytes 276488 | tf_op jit(solution)/shard_map/ppermute | solution.py:24
  20.5 3.3 %collective-permute-start.1 = (bf16[40,1152]{1,0:T(8,128)(2,1)S(1)}, bf16[40,1152]{1,0:T(8,128)(2,1)S(1)}, u32[]{:S(2)}, u32[]{:S(2)}) collective-permute-start(bf16[40,1152]{1,0:T(8,128)(2,1)S(1)} %get-tuple-element.20), channel_id=1, source_target_pairs={{0,64},{32,96},{64,128},{96,160},{128,192},{160,224},{192,0},{224,... | collective-permute-start | bytes 276488 | tf_op jit(solution)/shard_map/ppermute | solution.py:24
  23.7 4.0 %collective-permute-start.2 = (bf16[40,1152]{1,0:T(8,128)(2,1)S(1)}, bf16[40,1152]{1,0:T(8,128)(2,1)S(1)}, u32[]{:S(2)}, u32[]{:S(2)}) collective-permute-start(bf16[40,1152]{1,0:T(8,128)(2,1)S(1)} %get-tuple-element.20), channel_id=1, source_target_pairs={{0,96},{32,128},{64,160},{96,192},{128,224},{160,0},{192,32},{224,... | collective-permute-start | bytes 276488 | tf_op jit(solution)/shard_map/ppermute | solution.py:24
  28.3 4.9 %collective-permute-start.4 = (bf16[40,1152]{1,0:T(8,128)(2,1)S(1)}, bf16[40,1152]{1,0:T(8,128)(2,1)S(1)}, u32[]{:S(2)}, u32[]{:S(2)}) collective-permute-start(bf16[40,1152]{1,0:T(8,128)(2,1)S(1)} %get-tuple-element.20), channel_id=1, source_target_pairs={{0,160},{32,192},{64,224},{96,0},{128,32},{160,64},{192,96},{224,1... | collective-permute-start | bytes 276488 | tf_op jit(solution)/shard_map/ppermute | solution.py:24
  34.5 6.0 %all-to-all-start.1 = ((bf16[16,40,1152]{2,1,0:T(8,128)(2,1)}), bf16[16,40,1152]{2,1,0:T(8,128)(2,1)S(1)}, u32[]{:S(2)}, u32[]{:S(2)}) async-start(bf16[16,40,1152]{2,1,0:T(8,128)(2,1)} %broadcast_in_dim.22), calls=%async_computation.1 | async-start | bytes 2949120 | tf_op jit(solution)/shard_map/all_to_all | solution.py:16
  40.5 2.7 %collective-permute-start.5 = (bf16[40,1152]{1,0:T(8,128)(2,1)S(1)}, bf16[40,1152]{1,0:T(8,128)(2,1)S(1)}, u32[]{:S(2)}, u32[]{:S(2)}) collective-permute-start(bf16[40,1152]{1,0:T(8,128)(2,1)S(1)} %get-tuple-element.20), channel_id=1, source_target_pairs={{0,192},{32,224},{64,0},{96,32},{128,64},{160,96},{192,128},{224,1... | collective-permute-start | bytes 276488 | tf_op jit(solution)/shard_map/ppermute | solution.py:24
  51.6 7.4 %all-to-all-done.1 = bf16[16,40,1152]{2,1,0:T(8,128)(2,1)S(1)} async-done(((bf16[16,40,1152]{2,1,0:T(8,128)(2,1)}), bf16[16,40,1152]{2,1,0:T(8,128)(2,1)S(1)}, u32[]{:S(2)}, u32[]{:S(2)}) %all-to-all-start.1) | async-done | bytes 1474592 | tf_op jit(solution)/shard_map/all_to_all | solution.py:16
  59.0 2.0 %fusion.18 = bf16[640,320]{0,1:T(8,128)(2,1)S(1)} fusion(bf16[640,1152]{1,0:T(8,128)(2,1)S(1)} %bitcast.101, bf16[320,1152]{1,0:T(8,128)(2,1)} %collective-permute-done.7, f32[]{:T(128)} %bitcast.99, f32[]{:T(128)} %bitcast.6), kind=kOutput, calls=%fused_computation.32 | convolution fusion | flops 473292800 | bytes 2621448 | tf_op jit(solution)/shard_map/re,ce->rc/dot_general | solution.py:66
  60.9 1.7 convolution_convert_fusion
  62.6 2.2 %fusion.46 = f32[640,1152]{1,0:T(8,128)S(1)} fusion(bf16[640,320]{0,1:T(8,128)(2,1)S(1)} %fusion.18, bf16[320,1152]{1,0:T(8,128)(2,1)} %collective-permute-done.7), kind=kOutput, calls=%fused_computation.91 | convolution fusion | flops 471859200 | bytes 4096000 | tf_op jit(solution)/shard_map/dot_general | solution.py:85
  65.8 2.2 %fusion = bf16[640,1152]{1,0:T(8,128)(2,1)} fusion(f32[640,1152]{1,0:T(8,128)S(1)} %fusion.46, bf16[640,320]{0,1:T(8,128)(2,1)S(1)} %fusion.19, bf16[320,1152]{1,0:T(8,128)(2,1)S(1)} %copy-done.6), kind=kOutput, calls=%fused_computation.1 | convolution fusion | flops 473333760 | bytes 5570560 | tf_op jit(solution)/shard_map/dot_general | solution.py:84
  68.0 6.0 %all-to-all-start.2 = ((bf16[16,40,1152]{2,1,0:T(8,128)(2,1)}), bf16[16,40,1152]{2,1,0:T(8,128)(2,1)}, u32[]{:S(2)}, u32[]{:S(2)}) async-start(bf16[16,40,1152]{2,1,0:T(8,128)(2,1)} %bitcast.105), calls=%async_computation.2 | async-start | bytes 2949120 | tf_op jit(solution)/shard_map/all_to_all | solution.py:16
  74.0 1.9 %fusion.40 = (bf16[320,1152]{1,0:T(8,128)(2,1)S(1)}, f32[320,1152]{1,0:T(8,128)S(1)}) fusion(bf16[320,1152]{1,0:T(8,128)(2,1)} %collective-permute-done.8, bf16[640,320]{0,1:T(8,128)(2,1)S(1)} %fusion.19, bf16[640,1152]{1,0:T(8,128)(2,1)S(1)} %bitcast.104), kind=kOutput, calls=%fused_computation.85 | convolution fusion | flops 472965120 | bytes 4833280 | tf_op jit(solution)/shard_map/rc,re->ce/dot_general | solution.py:77
  76.0 2.7 %collective-permute-start.10 = (bf16[40,1152]{1,0:T(8,128)(2,1)S(1)}, bf16[40,1152]{1,0:T(8,128)(2,1)S(1)}, u32[]{:S(2)}, u32[]{:S(2)}) collective-permute-start(bf16[40,1152]{1,0:T(8,128)(2,1)S(1)} %get-tuple-element.15), channel_id=1, source_target_pairs={{0,192},{32,224},{64,0},{96,32},{128,64},{160,96},{192,128},{224,1... | collective-permute-start | bytes 276488 | tf_op jit(solution)/shard_map/ppermute | solution.py:24
  79.3 3.7 %collective-permute-start.12 = (bf16[40,1152]{1,0:T(8,128)(2,1)S(1)}, bf16[40,1152]{1,0:T(8,128)(2,1)S(1)}, u32[]{:S(2)}, u32[]{:S(2)}) collective-permute-start(bf16[40,1152]{1,0:T(8,128)(2,1)S(1)} %get-tuple-element.13), channel_id=1, source_target_pairs={{0,128},{32,160},{64,192},{96,224},{128,0},{160,32},{192,64},{224,... | collective-permute-start | bytes 276488 | tf_op jit(solution)/shard_map/ppermute | solution.py:24
  83.8 2.4 %collective-permute-start.14 = (bf16[40,1152]{1,0:T(8,128)(2,1)S(1)}, bf16[40,1152]{1,0:T(8,128)(2,1)S(1)}, u32[]{:S(2)}, u32[]{:S(2)}) collective-permute-start(bf16[40,1152]{1,0:T(8,128)(2,1)S(1)} %get-tuple-element.11), channel_id=1, source_target_pairs={{0,64},{32,96},{64,128},{96,160},{128,192},{160,224},{192,0},{224,... | collective-permute-start | bytes 276488 | tf_op jit(solution)/shard_map/ppermute | solution.py:24
  86.2 2.4 %collective-permute-start.15 = (bf16[40,1152]{1,0:T(8,128)(2,1)S(1)}, bf16[40,1152]{1,0:T(8,128)(2,1)S(1)}, u32[]{:S(2)}, u32[]{:S(2)}) collective-permute-start(bf16[40,1152]{1,0:T(8,128)(2,1)S(1)} %get-tuple-element.10), channel_id=1, source_target_pairs={{0,32},{32,64},{64,96},{96,128},{128,160},{160,192},{192,224},{224... | collective-permute-start | bytes 276488 | tf_op jit(solution)/shard_map/ppermute | solution.py:24
  88.6 4.4 %collective-permute-start.9 = (bf16[40,1152]{1,0:T(8,128)(2,1)S(1)}, bf16[40,1152]{1,0:T(8,128)(2,1)S(1)}, u32[]{:S(2)}, u32[]{:S(2)}) collective-permute-start(bf16[40,1152]{1,0:T(8,128)(2,1)S(1)} %get-tuple-element.9), channel_id=1, source_target_pairs={{0,224},{32,0},{64,32},{96,64},{128,96},{160,128},{192,160},{224,1... | collective-permute-start | bytes 276488 | tf_op jit(solution)/shard_map/ppermute | solution.py:24
  93.0 2.8 %collective-permute-done.13 = bf16[40,1152]{1,0:T(8,128)(2,1)S(1)} collective-permute-done((bf16[40,1152]{1,0:T(8,128)(2,1)S(1)}, bf16[40,1152]{1,0:T(8,128)(2,1)S(1)}, u32[]{:S(2)}, u32[]{:S(2)}) %collective-permute-start.13) | collective-permute-done | bytes 92192 | tf_op jit(solution)/shard_map/ppermute | solution.py:24
  95.8 4.3 %collective-permute-done.14 = bf16[40,1152]{1,0:T(8,128)(2,1)S(1)} collective-permute-done((bf16[40,1152]{1,0:T(8,128)(2,1)S(1)}, bf16[40,1152]{1,0:T(8,128)(2,1)S(1)}, u32[]{:S(2)}, u32[]{:S(2)}) %collective-permute-start.14) | collective-permute-done | bytes 92192 | tf_op jit(solution)/shard_map/ppermute | solution.py:24
  101.5 1.6 convert_reduce_fusion
  104.9 10.5 %all_to_all.31 = bf16[4,2,40,288]{3,2,1,0:T(8,128)(2,1)S(1)} all-to-all(bf16[4,2,40,288]{3,2,1,0:T(8,128)(2,1)S(1)} %copy.36), channel_id=1, replica_groups=mesh['z'=8,'xl'=2,'y'=4,'xh'=2,'c'=2] {'xh','c'}, dimensions={0} | all-to-all | bytes 368640 | tf_op jit(solution)/shard_map/all_to_all | solution.py:16
  118.2 1.6 stack.40
  120.6 1.4 copy.42
  122.0 5.8 %all-to-all-start.4 = ((bf16[8,288,288]{2,1,0:T(8,128)(2,1)}), bf16[8,288,288]{2,1,0:T(8,128)(2,1)}, u32[]{:S(2)}, u32[]{:S(2)}) async-start(bf16[8,288,288]{2,1,0:T(8,128)(2,1)} %copy.42), calls=%async_computation.4 | async-start | bytes 3538944 | tf_op jit(solution)/shard_map/all_to_all | solution.py:16
  133.2 3.0 %collective-permute-start.18 = (bf16[2,160,288]{2,1,0:T(8,128)(2,1)S(1)}, bf16[2,160,288]{2,1,0:T(8,128)(2,1)}, u32[]{:S(2)}, u32[]{:S(2)}) collective-permute-start(bf16[2,160,288]{2,1,0:T(8,128)(2,1)S(1)} %get-tuple-element.7), channel_id=1, source_target_pairs={{0,3},{1,2},{2,1},{3,0},{4,7},{5,6},{6,5},{7,4},{8,11},{9,10},{10,... | collective-permute-start | bytes 552968 | tf_op jit(solution)/shard_map/ppermute | solution.py:29
  136.2 13.7 %all-to-all-done.4 = bf16[8,288,288]{2,1,0:T(8,128)(2,1)} async-done(((bf16[8,288,288]{2,1,0:T(8,128)(2,1)}), bf16[8,288,288]{2,1,0:T(8,128)(2,1)}, u32[]{:S(2)}, u32[]{:S(2)}) %all-to-all-start.4) | async-done | bytes 1327136 | tf_op jit(solution)/shard_map/all_to_all | solution.py:16
  149.9 1.8 %reduce_sum.51 = bf16[288,288]{1,0:T(8,128)(2,1)S(1)} reduce(bf16[8,288,288]{2,1,0:T(8,128)(2,1)} %all-to-all-done.4, bf16[]{:T(256)} %constant.48.clone.1), dimensions={0}, to_apply=%region_3.4 | reduce | flops 580608 | bytes 1492994 | tf_op jit(solution)/shard_map/reduce_sum | solution.py:100
  152.7 4.1 %all-to-all-start.5 = ((bf16[8,2,18,288]{3,1,2,0:T(2,128)(2,1)}), bf16[8,2,18,288]{3,1,2,0:T(2,128)(2,1)S(1)}, u32[]{:S(2)}, u32[]{:S(2)}) async-start(bf16[8,2,18,288]{3,1,2,0:T(2,128)(2,1)} %copy.43), calls=%async_computation.5 | async-start | bytes 442368 | tf_op jit(solution)/shard_map/all_to_all | solution.py:16
  159.4 8.3 %all-to-all-done.5 = bf16[8,2,18,288]{3,1,2,0:T(2,128)(2,1)S(1)} async-done(((bf16[8,2,18,288]{3,1,2,0:T(2,128)(2,1)}), bf16[8,2,18,288]{3,1,2,0:T(2,128)(2,1)S(1)}, u32[]{:S(2)}, u32[]{:S(2)}) %all-to-all-start.5) | async-done | bytes 165920 | tf_op jit(solution)/shard_map/all_to_all | solution.py:16
  (91 shorter events, 31.2 us)
Async XLA Ops:
  0.6 1.0 copy-start
  0.6 2.5 %copy-start.5 = (bf16[160,1152]{1,0:T(8,128)(2,1)S(1)}, bf16[160,1152]{1,0:T(8,128)(2,1)}, u32[]{:S(2)}) copy-start(bf16[160,1152]{1,0:T(8,128)(2,1)} %param.7) | copy-start | bytes 1105924
  0.7 2.5 %copy-start.2 = (bf16[1152,288]{0,1:T(8,128)(2,1)S(1)}, bf16[1152,288]{0,1:T(8,128)(2,1)}, u32[]{:S(2)}) copy-start(bf16[1152,288]{0,1:T(8,128)(2,1)} %param.9) | copy-start | bytes 1990660
  17.8 22.6 %collective-permute-start = (bf16[40,1152]{1,0:T(8,128)(2,1)S(1)}, bf16[40,1152]{1,0:T(8,128)(2,1)S(1)}, u32[]{:S(2)}, u32[]{:S(2)}) collective-permute-start(bf16[40,1152]{1,0:T(8,128)(2,1)S(1)} %get-tuple-element.20), channel_id=1, source_target_pairs={{0,32},{32,64},{64,96},{96,128},{128,160},{160,192},{192,224},{224... | collective-permute-start | bytes 276488 | tf_op jit(solution)/shard_map/ppermute | solution.py:24
  20.5 23.4 %collective-permute-start.1 = (bf16[40,1152]{1,0:T(8,128)(2,1)S(1)}, bf16[40,1152]{1,0:T(8,128)(2,1)S(1)}, u32[]{:S(2)}, u32[]{:S(2)}) collective-permute-start(bf16[40,1152]{1,0:T(8,128)(2,1)S(1)} %get-tuple-element.20), channel_id=1, source_target_pairs={{0,64},{32,96},{64,128},{96,160},{128,192},{160,224},{192,0},{224,... | collective-permute-start | bytes 276488 | tf_op jit(solution)/shard_map/ppermute | solution.py:24
  23.7 21.8 %collective-permute-start.2 = (bf16[40,1152]{1,0:T(8,128)(2,1)S(1)}, bf16[40,1152]{1,0:T(8,128)(2,1)S(1)}, u32[]{:S(2)}, u32[]{:S(2)}) collective-permute-start(bf16[40,1152]{1,0:T(8,128)(2,1)S(1)} %get-tuple-element.20), channel_id=1, source_target_pairs={{0,96},{32,128},{64,160},{96,192},{128,224},{160,0},{192,32},{224,... | collective-permute-start | bytes 276488 | tf_op jit(solution)/shard_map/ppermute | solution.py:24
  27.8 18.4 %collective-permute-start.3 = (bf16[40,1152]{1,0:T(8,128)(2,1)S(1)}, bf16[40,1152]{1,0:T(8,128)(2,1)S(1)}, u32[]{:S(2)}, u32[]{:S(2)}) collective-permute-start(bf16[40,1152]{1,0:T(8,128)(2,1)S(1)} %get-tuple-element.20), channel_id=1, source_target_pairs={{0,128},{32,160},{64,192},{96,224},{128,0},{160,32},{192,64},{224,... | collective-permute-start | bytes 276488 | tf_op jit(solution)/shard_map/ppermute | solution.py:24
  28.3 18.5 %collective-permute-start.4 = (bf16[40,1152]{1,0:T(8,128)(2,1)S(1)}, bf16[40,1152]{1,0:T(8,128)(2,1)S(1)}, u32[]{:S(2)}, u32[]{:S(2)}) collective-permute-start(bf16[40,1152]{1,0:T(8,128)(2,1)S(1)} %get-tuple-element.20), channel_id=1, source_target_pairs={{0,160},{32,192},{64,224},{96,0},{128,32},{160,64},{192,96},{224,1... | collective-permute-start | bytes 276488 | tf_op jit(solution)/shard_map/ppermute | solution.py:24
  34.5 24.5 %all-to-all-start.1 = ((bf16[16,40,1152]{2,1,0:T(8,128)(2,1)}), bf16[16,40,1152]{2,1,0:T(8,128)(2,1)S(1)}, u32[]{:S(2)}, u32[]{:S(2)}) async-start(bf16[16,40,1152]{2,1,0:T(8,128)(2,1)} %broadcast_in_dim.22), calls=%async_computation.1 | async-start | bytes 2949120 | tf_op jit(solution)/shard_map/all_to_all | solution.py:16
  40.5 7.0 %collective-permute-start.5 = (bf16[40,1152]{1,0:T(8,128)(2,1)S(1)}, bf16[40,1152]{1,0:T(8,128)(2,1)S(1)}, u32[]{:S(2)}, u32[]{:S(2)}) collective-permute-start(bf16[40,1152]{1,0:T(8,128)(2,1)S(1)} %get-tuple-element.20), channel_id=1, source_target_pairs={{0,192},{32,224},{64,0},{96,32},{128,64},{160,96},{192,128},{224,1... | collective-permute-start | bytes 276488 | tf_op jit(solution)/shard_map/ppermute | solution.py:24
  43.9 4.6 %collective-permute-start.6 = (bf16[40,1152]{1,0:T(8,128)(2,1)S(1)}, bf16[40,1152]{1,0:T(8,128)(2,1)S(1)}, u32[]{:S(2)}, u32[]{:S(2)}) collective-permute-start(bf16[40,1152]{1,0:T(8,128)(2,1)S(1)} %get-tuple-element.20), channel_id=1, source_target_pairs={{0,224},{32,0},{64,32},{96,64},{128,96},{160,128},{192,160},{224,1... | collective-permute-start | bytes 276488 | tf_op jit(solution)/shard_map/ppermute | solution.py:24
  49.0 2.6 %collective-permute-start.7 = (bf16[320,1152]{1,0:T(8,128)(2,1)}, bf16[320,1152]{1,0:T(8,128)(2,1)}, u32[]{:S(2)}, u32[]{:S(2)}) collective-permute-start(bf16[320,1152]{1,0:T(8,128)(2,1)} %constant_dynamic-update-slice_fusion), channel_id=1, source_target_pairs={{0,1},{1,0},{2,3},{3,2},{4,5},{5,4},{6,7},{7,6},{8,9},{9,8},{10,11... | collective-permute-start | bytes 2211848 | tf_op jit(solution)/shard_map/ppermute | solution.py:20
  62.6 2.2 %copy-start.6 = (bf16[320,1152]{1,0:T(8,128)(2,1)S(1)}, bf16[320,1152]{1,0:T(8,128)(2,1)}, u32[]{:S(2)}) copy-start(bf16[320,1152]{1,0:T(8,128)(2,1)} %constant_dynamic-update-slice_fusion) | copy-start | bytes 2211844
  62.6 11.4 %collective-permute-start.8 = (bf16[320,1152]{1,0:T(8,128)(2,1)}, bf16[320,1152]{1,0:T(8,128)(2,1)}, u32[]{:S(2)}, u32[]{:S(2)}) collective-permute-start(bf16[320,1152]{1,0:T(8,128)(2,1)} %convolution_convert_fusion), channel_id=1, source_target_pairs={{0,1},{1,0},{2,3},{3,2},{4,5},{5,4},{6,7},{7,6},{8,9},{9,8},{10,11... | collective-permute-start | bytes 2211848 | tf_op jit(solution)/shard_map/ppermute | solution.py:20
  68.0 33.5 %all-to-all-start.2 = ((bf16[16,40,1152]{2,1,0:T(8,128)(2,1)}), bf16[16,40,1152]{2,1,0:T(8,128)(2,1)}, u32[]{:S(2)}, u32[]{:S(2)}) async-start(bf16[16,40,1152]{2,1,0:T(8,128)(2,1)} %bitcast.105), calls=%async_computation.2 | async-start | bytes 2949120 | tf_op jit(solution)/shard_map/all_to_all | solution.py:16
  76.0 10.2 %collective-permute-start.10 = (bf16[40,1152]{1,0:T(8,128)(2,1)S(1)}, bf16[40,1152]{1,0:T(8,128)(2,1)S(1)}, u32[]{:S(2)}, u32[]{:S(2)}) collective-permute-start(bf16[40,1152]{1,0:T(8,128)(2,1)S(1)} %get-tuple-element.15), channel_id=1, source_target_pairs={{0,192},{32,224},{64,0},{96,32},{128,64},{160,96},{192,128},{224,1... | collective-permute-start | bytes 276488 | tf_op jit(solution)/shard_map/ppermute | solution.py:24
  78.7 9.9 %collective-permute-start.11 = (bf16[40,1152]{1,0:T(8,128)(2,1)S(1)}, bf16[40,1152]{1,0:T(8,128)(2,1)S(1)}, u32[]{:S(2)}, u32[]{:S(2)}) collective-permute-start(bf16[40,1152]{1,0:T(8,128)(2,1)S(1)} %get-tuple-element.14), channel_id=1, source_target_pairs={{0,160},{32,192},{64,224},{96,0},{128,32},{160,64},{192,96},{224,1... | collective-permute-start | bytes 276488 | tf_op jit(solution)/shard_map/ppermute | solution.py:24
  79.3 13.7 %collective-permute-start.12 = (bf16[40,1152]{1,0:T(8,128)(2,1)S(1)}, bf16[40,1152]{1,0:T(8,128)(2,1)S(1)}, u32[]{:S(2)}, u32[]{:S(2)}) collective-permute-start(bf16[40,1152]{1,0:T(8,128)(2,1)S(1)} %get-tuple-element.13), channel_id=1, source_target_pairs={{0,128},{32,160},{64,192},{96,224},{128,0},{160,32},{192,64},{224,... | collective-permute-start | bytes 276488 | tf_op jit(solution)/shard_map/ppermute | solution.py:24
  83.0 12.8 %collective-permute-start.13 = (bf16[40,1152]{1,0:T(8,128)(2,1)S(1)}, bf16[40,1152]{1,0:T(8,128)(2,1)S(1)}, u32[]{:S(2)}, u32[]{:S(2)}) collective-permute-start(bf16[40,1152]{1,0:T(8,128)(2,1)S(1)} %get-tuple-element.12), channel_id=1, source_target_pairs={{0,96},{32,128},{64,160},{96,192},{128,224},{160,0},{192,32},{224,... | collective-permute-start | bytes 276488 | tf_op jit(solution)/shard_map/ppermute | solution.py:24
  83.8 16.3 %collective-permute-start.14 = (bf16[40,1152]{1,0:T(8,128)(2,1)S(1)}, bf16[40,1152]{1,0:T(8,128)(2,1)S(1)}, u32[]{:S(2)}, u32[]{:S(2)}) collective-permute-start(bf16[40,1152]{1,0:T(8,128)(2,1)S(1)} %get-tuple-element.11), channel_id=1, source_target_pairs={{0,64},{32,96},{64,128},{96,160},{128,192},{160,224},{192,0},{224,... | collective-permute-start | bytes 276488 | tf_op jit(solution)/shard_map/ppermute | solution.py:24
  86.2 15.0 %collective-permute-start.15 = (bf16[40,1152]{1,0:T(8,128)(2,1)S(1)}, bf16[40,1152]{1,0:T(8,128)(2,1)S(1)}, u32[]{:S(2)}, u32[]{:S(2)}) collective-permute-start(bf16[40,1152]{1,0:T(8,128)(2,1)S(1)} %get-tuple-element.10), channel_id=1, source_target_pairs={{0,32},{32,64},{64,96},{96,128},{128,160},{160,192},{192,224},{224... | collective-permute-start | bytes 276488 | tf_op jit(solution)/shard_map/ppermute | solution.py:24
  88.6 12.6 %collective-permute-start.9 = (bf16[40,1152]{1,0:T(8,128)(2,1)S(1)}, bf16[40,1152]{1,0:T(8,128)(2,1)S(1)}, u32[]{:S(2)}, u32[]{:S(2)}) collective-permute-start(bf16[40,1152]{1,0:T(8,128)(2,1)S(1)} %get-tuple-element.9), channel_id=1, source_target_pairs={{0,224},{32,0},{64,32},{96,64},{128,96},{160,128},{192,160},{224,1... | collective-permute-start | bytes 276488 | tf_op jit(solution)/shard_map/ppermute | solution.py:24
  122.0 5.8 %copy-start.3 = (bf16[1152,288]{0,1:T(8,128)(2,1)S(1)}, bf16[1152,288]{0,1:T(8,128)(2,1)}, u32[]{:S(2)}) copy-start(bf16[1152,288]{0,1:T(8,128)(2,1)} %param.9) | copy-start | bytes 1990660
  122.0 27.9 %all-to-all-start.4 = ((bf16[8,288,288]{2,1,0:T(8,128)(2,1)}), bf16[8,288,288]{2,1,0:T(8,128)(2,1)}, u32[]{:S(2)}, u32[]{:S(2)}) async-start(bf16[8,288,288]{2,1,0:T(8,128)(2,1)} %copy.42), calls=%async_computation.4 | async-start | bytes 3538944 | tf_op jit(solution)/shard_map/all_to_all | solution.py:16
  127.9 1.1 copy-start.4
  130.2 1.2 copy-start.1
  132.8 24.0 %collective-permute-start.16 = (bf16[2,160,288]{2,1,0:T(8,128)(2,1)}, bf16[2,160,288]{2,1,0:T(8,128)(2,1)}, u32[]{:S(2)}, u32[]{:S(2)}) collective-permute-start(bf16[2,160,288]{2,1,0:T(8,128)(2,1)} %get-tuple-element.6), channel_id=1, source_target_pairs={{0,1},{1,0},{2,3},{3,2},{4,5},{5,4},{6,7},{7,6},{8,9},{9,8},{10,11... | collective-permute-start | bytes 552968 | tf_op jit(solution)/shard_map/ppermute | solution.py:29
  132.8 24.0 %collective-permute-start.17 = (bf16[2,160,288]{2,1,0:T(8,128)(2,1)S(1)}, bf16[2,160,288]{2,1,0:T(8,128)(2,1)}, u32[]{:S(2)}, u32[]{:S(2)}) collective-permute-start(bf16[2,160,288]{2,1,0:T(8,128)(2,1)S(1)} %get-tuple-element.8), channel_id=1, source_target_pairs={{0,2},{1,3},{2,0},{3,1},{4,6},{5,7},{6,4},{7,5},{8,10},{9,11},{10,... | collective-permute-start | bytes 552968 | tf_op jit(solution)/shard_map/ppermute | solution.py:29
  133.2 24.1 %collective-permute-start.18 = (bf16[2,160,288]{2,1,0:T(8,128)(2,1)S(1)}, bf16[2,160,288]{2,1,0:T(8,128)(2,1)}, u32[]{:S(2)}, u32[]{:S(2)}) collective-permute-start(bf16[2,160,288]{2,1,0:T(8,128)(2,1)S(1)} %get-tuple-element.7), channel_id=1, source_target_pairs={{0,3},{1,2},{2,1},{3,0},{4,7},{5,6},{6,5},{7,4},{8,11},{9,10},{10,... | collective-permute-start | bytes 552968 | tf_op jit(solution)/shard_map/ppermute | solution.py:29
  152.7 15.0 %all-to-all-start.5 = ((bf16[8,2,18,288]{3,1,2,0:T(2,128)(2,1)}), bf16[8,2,18,288]{3,1,2,0:T(2,128)(2,1)S(1)}, u32[]{:S(2)}, u32[]{:S(2)}) async-start(bf16[8,2,18,288]{3,1,2,0:T(2,128)(2,1)} %copy.43), calls=%async_computation.5 | async-start | bytes 442368 | tf_op jit(solution)/shard_map/all_to_all | solution.py:16

commit v3 on v2

--- a/solution.py
+++ b/solution.py
@@ -29,37 +29,52 @@
     return lax.ppermute(x, MP, pairs)
 
 
-def rows_from_slices(pair):
-    n = pair.shape[1] // 4
-    parts = a2a(pair.reshape(2, 4, n, 288).transpose(1, 0, 2, 3), MP)
-    return parts.transpose(1, 2, 0, 3).reshape(2, n, 1152)
-
-
-def slices_from_rows(pair):
-    n = pair.shape[1]
-    parts = a2a(pair.reshape(2, n, 4, 288).transpose(2, 0, 1, 3), MP)
-    return parts.transpose(1, 0, 2, 3).reshape(2, 4 * n, 288)
+def rows_from_slices(pair, xh, c):
+    quarters = pair.reshape(2, 2, 2, 40, 288)
+    got = {}
+    for dx in range(2):
+        for dc in range(2):
+            to = lax.dynamic_index_in_dim(quarters, xh ^ dx, 1, keepdims=False)
+            to = lax.dynamic_index_in_dim(to, c ^ dc, 1, keepdims=False)
+            got[dx, dc] = mp_shift(to, dx, dc) if dx or dc else to
+    parts = []
+    for a in range(2):
+        for b in range(2):
+            near = jnp.where(c == b, got[0, 0], got[0, 1])
+            far = jnp.where(c == b, got[1, 0], got[1, 1])
+            parts.append(jnp.where(xh == a, near, far))
+    return jnp.concatenate(parts, axis=2)
 
 
 def shards(image_features, text_features, image_proj, text_proj, log_scale, bias):
+    zi = lax.axis_index("z")
     xl, y, xh, c = (lax.axis_index(a) for a in AXES[1:])
+    both = jnp.concatenate(
+        [
+            feats.reshape(160, 8, 8, 18).transpose(2, 0, 1, 3).reshape(8, 160, 144)
+            for feats in (image_features, text_features)
+        ],
+        axis=2,
+    )
+    plane_features = a2a(both, ("xl", "y")).reshape(1280, 288)
     p_img = jnp.dot(image_features, image_proj, preferred_element_type=F32)
     p_txt = jnp.dot(text_features, text_proj, preferred_element_type=F32)
-    own = rows_from_slices(jnp.stack([p_img, p_txt]))
+    own = rows_from_slices(jnp.stack([p_img, p_txt]), xh, c)
     r = lax.rsqrt(jnp.sum(own * own, axis=2, keepdims=True) + 1e-06)
     z = (own * r).astype(BF)
+    z, plane_features = lax.optimization_barrier((z, plane_features))
     z_img, z_txt = z[0], z[1]
     r_img, r_txt = r[0], r[1]
 
     img = a2a(jnp.broadcast_to(z_img[None], (16, 40, 1152)), PLANE).reshape(640, 1152)
-    txt_own = jnp.concatenate([z_txt] + [shift(z_txt, "z", 8, d) for d in range(1, 8)])
+    txt_own = lax.all_gather(z_txt, "z", axis=0, tiled=True)
     txt_oth = swap_core(txt_own)
 
     scale = jnp.exp(log_scale[0])
     offset = bias[0]
     place = (xl * 4 + y) * 2 + xh
     row_ids = jnp.arange(640, dtype=jnp.int32)[:, None] - place * 40
-    col_ids = jnp.arange(320, dtype=jnp.int32)[None, :]
+    col_ids = jnp.arange(320, dtype=jnp.int32)[None, :] - zi * 40
     diag = (row_ids == col_ids) & (row_ids >= 0) & (row_ids < 40)
 
     def coefs(txt, mask):
@@ -76,10 +91,12 @@
     t_got = swap_core(t_oth)
     t_own = jnp.einsum("rc,re->ce", coef_own, img, preferred_element_type=F32)
     t_sum = t_own + t_got.astype(F32)
-    t_out = t_sum[40:].astype(BF)
-    gz_txt = t_sum[:40]
+    t_sum = t_sum.reshape(8, 40, 1152)
+    gz_txt = lax.dynamic_index_in_dim(t_sum, zi, 0, keepdims=False)
+    t_out = t_sum.astype(BF)
     for d in range(1, 8):
-        gz_txt = gz_txt + shift(t_out[40 * d - 40 : 40 * d], "z", 8, -d).astype(F32)
+        piece = lax.dynamic_index_in_dim(t_out, (zi + d) % 8, 0, keepdims=False)
+        gz_txt = gz_txt + shift(piece, "z", 8, d).astype(F32)
     g_img = (
         jnp.dot(coef_own, txt_own, preferred_element_type=F32)
         + jnp.dot(coef_oth, txt_oth, preferred_element_type=F32)
@@ -90,17 +107,22 @@
     values = z.astype(F32)
     inner = jnp.sum(values * gz, axis=2, keepdims=True)
     gp_rows = (r * (gz - values * inner)).astype(BF)
-    gp = slices_from_rows(gp_rows)
-    gp_img, gp_txt = gp[0], gp[1]
-
-    w_img = jnp.einsum("rd,re->de", image_features, gp_img, preferred_element_type=F32)
-    w_txt = jnp.einsum("rd,re->de", text_features, gp_txt, preferred_element_type=F32)
-    w = jnp.stack([w_img, w_txt]).astype(BF).reshape(2, 8, 8, 18, 288)
-    w = w.transpose(2, 0, 1, 3, 4).reshape(8, 2 * 144, 288)
-    w = jnp.sum(a2a(w, ("xl", "y")).astype(F32), axis=0).astype(BF)
-    w = w.reshape(2, 8, 18, 288).transpose(1, 0, 2, 3)
+    cut = gp_rows.reshape(2, 40, 4, 288).transpose(2, 0, 1, 3)
+    rest = jnp.concatenate([cut[:, 0, :, 256:], cut[:, 1, :, 256:], jnp.zeros((4, 40, 64), BF)], axis=2)
+    piece = jnp.concatenate(
+        [cut[:, :, :, :128].reshape(4, 80, 128), cut[:, :, :, 128:256].reshape(4, 80, 128), rest], axis=1
+    )
+    got = a2a(jnp.broadcast_to(piece[None], (8, 4, 200, 128)).reshape(32, 200, 128), ("xl", "y", "xh", "c"))
+    cols = [got[:, 40 * i : 40 * i + 40].reshape(1280, 128) for i in (0, 2, 1, 3, 4)]
+    w = jnp.einsum("rd,re->de", plane_features, jnp.concatenate(cols, axis=1), preferred_element_type=F32)
+    w = jnp.stack([jnp.concatenate([w[:144, :256], w[:144, 512:544]], axis=1), jnp.concatenate([w[144:, 256:512], w[144:, 544:576]], axis=1)])
+    w = w.astype(BF).reshape(2, 8, 18, 288).transpose(1, 0, 2, 3)
     w = jnp.sum(a2a(w, ("z",)).astype(F32), axis=0)
 
+    mine = lax.dynamic_slice_in_dim(got, (xl * 4 + y) * 4, 4, 0)
+    mine = [mine[:, 40 * i : 40 * i + 40].reshape(160, 128) for i in range(5)]
+    gp_img = jnp.concatenate([mine[0], mine[2], mine[4][:, :32]], axis=1)
+    gp_txt = jnp.concatenate([mine[1], mine[3], mine[4][:, 32:64]], axis=1)
     f_img = jnp.einsum("re,de->rd", gp_img, image_proj, preferred_element_type=F32)
     f_txt = jnp.einsum("re,de->rd", gp_txt, text_proj, preferred_element_type=F32)
     f = jnp.stack([f_img, f_txt]).reshape(2, 160, 4, 288).transpose(2, 0, 1, 3)

time: 170 us -> 187 us (1.10)
  waiting for transfers between devices: 39.5 us -> 51.9 us
  blocking collectives: 23.7 us -> 31.6 us
  starting transfers between devices: 60.9 us -> 54.2 us
  matrix products: 14.6 us -> 18.8 us
  local copies, waits for them, and re-layouts: 20.5 us -> 17.3 us
    all_gather x0 -> x1, blocking collectives: none -> 31.6 us  [shards(): txt_own = lax.all_gather(z_txt, 'z', axis=0, tiled=True)]
    all_to_all x2 -> x0, blocking collectives: 23.7 us -> none  [a2a(): return lax.all_to_all(x, axes, 0, 0, tiled=True)]
    ppermute x14 -> x7, starting transfers between devices: 35.5 us -> 14.6 us  [shift(): return lax.ppermute(x, axis, [(i, (i + step) % size) for i in range(size)])]
    all_to_all x4 -> x5, starting transfers between devices: 22 us -> 32.1 us  [a2a(): return lax.all_to_all(x, axes, 0, 0, tiled=True)]
    all_to_all x4 -> x5, waiting for transfers between devices: 29.4 us -> 37.2 us  [a2a(): return lax.all_to_all(x, axes, 0, 0, tiled=True)]
    ppermute x3 -> x6, waiting for transfers between devices: 0.4 us -> 4.81 us  [mp_shift(): return lax.ppermute(x, MP, pairs)]
    ppermute x3 -> x6, starting transfers between devices: 3.36 us -> 7.29 us  [mp_shift(): return lax.ppermute(x, MP, pairs)]
    unnamed x24 -> x33, local copies, waits for them, and re-layouts: 8.09 us -> 4.35 us
  transfers between devices with their start and end apart: 23 -> 20, of which waited for: 9 -> 7; matrix products, arithmetic and copies ran while one was open for 13% -> 11% of each run, Pallas kernels for 0% -> 0%
where the time goes in v3:
time: 187 us; the launch traced here: 185 us
  starting transfers between devices  54.2 us (29%)
  waiting for transfers between devices  51.9 us (28%)
  blocking collectives  31.6 us (17%)
  matrix products  18.8 us (10%)
  local copies, waits for them, and re-layouts  17.3 us (9%)
  other arithmetic  9.18 us (5%)
  between operations  2.53 us (1%)
    all_to_all x5, waiting for transfers between devices, a2a(): return lax.all_to_all(x, axes, 0, 0, tiled=True)  37.2 us
    all_to_all x5, starting transfers between devices, a2a(): return lax.all_to_all(x, axes, 0, 0, tiled=True)  32.1 us
    all_gather x1, blocking collectives, shards(): txt_own = lax.all_gather(z_txt, 'z', axis=0, tiled=True)  31.6 us
    ppermute x7, starting transfers between devices, shift(): return lax.ppermute(x, axis, [(i, (i + step) % size) for i in range(size)])  14.6 us
    ppermute x7, waiting for transfers between devices, shift(): return lax.ppermute(x, axis, [(i, (i + step) % size) for i in range(size)])  8.7 us
    ppermute x6, starting transfers between devices, mp_shift(): return lax.ppermute(x, MP, pairs)  7.29 us
    ppermute x6, waiting for transfers between devices, mp_shift(): return lax.ppermute(x, MP, pairs)  4.81 us
    dot_general x2, matrix products, coefs(): d = jnp.einsum('re,ce->rc', img, txt, preferred_element_type=F32)  4.51 us
  transfers between devices with their start and end apart: 20, of which 7 were waited for; matrix products, arithmetic and copies ran while one was open for 11% of the time, Pallas kernels for 0%

profile of v3, /device:TPU:2, one launch (start us, length us, event | category | flops | bytes accessed | tf_op | source)
XLA Modules:
  0.0 185.4 jit_solution(4696083644707706622)
XLA Ops:
  0.7 1.7 fusion.68
  2.4 1.5 fusion.69
  4.7 1.6 collective-permute-start.2
  7.0 1.4 collective-permute-start.1
  9.8 1.6 copy.46
  11.4 5.9 %all-to-all-start = ((bf16[8,160,288]{2,1,0:T(8,128)(2,1)}), bf16[8,160,288]{2,1,0:T(8,128)(2,1)S(1)}, u32[]{:S(2)}, u32[]{:S(2)}) async-start(bf16[8,160,288]{2,1,0:T(8,128)(2,1)} %copy.46), calls=%async_computation | async-start | bytes 1966080 | tf_op jit(solution)/shard_map/all_to_all | solution.py:16
  19.9 11.0 %all-to-all-done = bf16[8,160,288]{2,1,0:T(8,128)(2,1)S(1)} async-done(((bf16[8,160,288]{2,1,0:T(8,128)(2,1)}), bf16[8,160,288]{2,1,0:T(8,128)(2,1)S(1)}, u32[]{:S(2)}, u32[]{:S(2)}) %all-to-all-start) | async-done | bytes 737312 | tf_op jit(solution)/shard_map/all_to_all | solution.py:16
  32.1 5.7 %all-to-all-start.1 = ((bf16[16,40,1152]{2,1,0:T(8,128)(2,1)}), bf16[16,40,1152]{2,1,0:T(8,128)(2,1)S(1)}, u32[]{:S(2)}, u32[]{:S(2)}) async-start(bf16[16,40,1152]{2,1,0:T(8,128)(2,1)} %broadcast_in_dim.31), calls=%async_computation.1 | async-start | bytes 2949120 | tf_op jit(solution)/shard_map/all_to_all | solution.py:16
  37.9 31.6 %all-gather = bf16[1,320,1152]{2,1,0:T(8,128)(2,1)} all-gather(bf16[1,40,1152]{2,1,0:T(8,128)(2,1)S(1)} %get-tuple-element.46), channel_id=2, replica_groups=mesh['z'=8,'xl'=2,'y'=4,'xh'=2,'c'=2] {'z'}, dimensions={1}, use_global_device_ids=true | all-gather | bytes 829440 | tf_op jit(solution)/shard_map/all_gather | solution.py:70
  72.0 2.5 %fusion.20 = bf16[640,320]{0,1:T(8,128)(2,1)S(1)} fusion(bf16[640,1152]{1,0:T(8,128)(2,1)S(1)} %bitcast.130, bf16[320,1152]{1,0:T(8,128)(2,1)} %collective-permute-done.3, f32[]{:T(128)} %bitcast.126, f32[]{:T(128)} %bitcast.6), kind=kOutput, calls=%fused_computation.26 | convolution fusion | flops 473292800 | bytes 2621448 | tf_op jit(solution)/shard_map/re,ce->rc/dot_general | solution.py:81
  74.5 1.7 convolution_convert_fusion
  76.3 2.0 %fusion.21 = bf16[640,320]{0,1:T(8,128)(2,1)S(1)} fusion(bf16[640,1152]{1,0:T(8,128)(2,1)S(1)} %bitcast.132, f32[]{:T(128)} %bitcast.125, f32[]{:T(128)} %bitcast.6, s32[640]{0:T(1024)S(1)} %iota_subtract_fusion, s32[320]{0:T(512)S(1)} %iota_subtract_fusion.1, pred[640]{0:T(1024)(128)(4,1)S(1)} %get-tuple-element.52, ...), kind=kOutput, calls=%fused_computation.27 | convolution fusion | flops 474726400 | bytes 2626568 | tf_op jit(solution)/shard_map/re,ce->rc/dot_general | solution.py:81
  79.1 2.1 %fusion.57 = f32[640,1152]{1,0:T(8,128)S(1)} fusion(bf16[640,320]{0,1:T(8,128)(2,1)S(1)} %fusion.21, bf16[1,320,1152]{2,1,0:T(8,128)(2,1)} %all-gather), kind=kOutput, calls=%fused_computation.124 | convolution fusion | flops 471859200 | bytes 4096000 | tf_op jit(solution)/shard_map/dot_general | solution.py:101
  81.3 3.3 %fusion.1 = bf16[640,1152]{1,0:T(8,128)(2,1)} fusion(f32[640,1152]{1,0:T(8,128)S(1)} %fusion.57, bf16[640,320]{0,1:T(8,128)(2,1)S(1)} %fusion.20, bf16[320,1152]{1,0:T(8,128)(2,1)} %collective-permute-done.3), kind=kOutput, calls=%fused_computation.2 | convolution fusion | flops 473333760 | bytes 5570560 | tf_op jit(solution)/shard_map/dot_general | solution.py:102
  84.6 7.4 %all-to-all-start.2 = ((bf16[16,40,1152]{2,1,0:T(8,128)(2,1)}), bf16[16,40,1152]{2,1,0:T(8,128)(2,1)}, u32[]{:S(2)}, u32[]{:S(2)}) async-start(bf16[16,40,1152]{2,1,0:T(8,128)(2,1)} %bitcast.16), calls=%async_computation.2 | async-start | bytes 2949120 | tf_op jit(solution)/shard_map/all_to_all | solution.py:16
  91.9 2.5 %convert_add_fusion = f32[320,1152]{1,0:T(8,128)S(1)} fusion(bf16[320,1152]{1,0:T(8,128)(2,1)} %collective-permute-done.4, bf16[640,320]{0,1:T(8,128)(2,1)} %copy-done.3, bf16[640,1152]{1,0:T(8,128)(2,1)} %bitcast.133), kind=kOutput, calls=%fused_computation.9 | convolution fusion | flops 472596480 | bytes 4096000 | tf_op jit(solution)/shard_map/rc,re->ce/dot_general | solution.py:92
  96.3 2.3 %collective-permute-start.11 = (bf16[40,1152]{1,0:T(8,128)(2,1)S(1)}, bf16[40,1152]{1,0:T(8,128)(2,1)}, u32[]{:S(2)}, u32[]{:S(2)}) collective-permute-start(bf16[40,1152]{1,0:T(8,128)(2,1)S(1)} %get-tuple-element.24), channel_id=1, source_target_pairs={{0,224},{32,0},{64,32},{96,64},{128,96},{160,128},{192,160},{224,1... | collective-permute-start | bytes 276488 | tf_op jit(solution)/shard_map/ppermute | solution.py:24
  98.9 3.1 %collective-permute-start.9 = (bf16[40,1152]{1,0:T(8,128)(2,1)}, bf16[40,1152]{1,0:T(8,128)(2,1)S(1)}, u32[]{:S(2)}, u32[]{:S(2)}) collective-permute-start(bf16[40,1152]{1,0:T(8,128)(2,1)} %get-tuple-element.26), channel_id=1, source_target_pairs={{0,160},{32,192},{64,224},{96,0},{128,32},{160,64},{192,96},{224,1... | collective-permute-start | bytes 276488 | tf_op jit(solution)/shard_map/ppermute | solution.py:24
  102.0 3.4 %collective-permute-start.8 = (bf16[40,1152]{1,0:T(8,128)(2,1)}, bf16[40,1152]{1,0:T(8,128)(2,1)}, u32[]{:S(2)}, u32[]{:S(2)}) collective-permute-start(bf16[40,1152]{1,0:T(8,128)(2,1)} %get-tuple-element.27), channel_id=1, source_target_pairs={{0,128},{32,160},{64,192},{96,224},{128,0},{160,32},{192,64},{224,... | collective-permute-start | bytes 276488 | tf_op jit(solution)/shard_map/ppermute | solution.py:24
  106.0 3.9 %collective-permute-start.6 = (bf16[40,1152]{1,0:T(8,128)(2,1)}, bf16[40,1152]{1,0:T(8,128)(2,1)}, u32[]{:S(2)}, u32[]{:S(2)}) collective-permute-start(bf16[40,1152]{1,0:T(8,128)(2,1)} %get-tuple-element.29), channel_id=1, source_target_pairs={{0,64},{32,96},{64,128},{96,160},{128,192},{160,224},{192,0},{224,... | collective-permute-start | bytes 276488 | tf_op jit(solution)/shard_map/ppermute | solution.py:24
  110.1 5.1 %collective-permute-done.8 = bf16[40,1152]{1,0:T(8,128)(2,1)} collective-permute-done((bf16[40,1152]{1,0:T(8,128)(2,1)}, bf16[40,1152]{1,0:T(8,128)(2,1)}, u32[]{:S(2)}, u32[]{:S(2)}) %collective-permute-start.8) | collective-permute-done | bytes 92192 | tf_op jit(solution)/shard_map/ppermute | solution.py:24
  115.2 3.6 %collective-permute-done.7 = bf16[40,1152]{1,0:T(8,128)(2,1)} collective-permute-done((bf16[40,1152]{1,0:T(8,128)(2,1)}, bf16[40,1152]{1,0:T(8,128)(2,1)}, u32[]{:S(2)}, u32[]{:S(2)}) %collective-permute-start.7) | collective-permute-done | bytes 92192 | tf_op jit(solution)/shard_map/ppermute | solution.py:24
  120.0 1.6 convert_reduce_fusion
  123.3 1.4 broadcast_in_dim.33
  124.7 7.4 %all-to-all-start.3 = ((bf16[32,200,128]{2,1,0:T(8,128)(2,1)}), bf16[32,200,128]{2,1,0:T(8,128)(2,1)S(1)}, u32[]{:S(2)}, u32[]{:S(2)}) async-start(bf16[32,200,128]{2,1,0:T(8,128)(2,1)} %bitcast.129), calls=%async_computation.3 | async-start | bytes 3276800 | tf_op jit(solution)/shard_map/all_to_all | solution.py:16
  132.1 22.2 %all-to-all-done.3 = bf16[32,200,128]{2,1,0:T(8,128)(2,1)S(1)} async-done(((bf16[32,200,128]{2,1,0:T(8,128)(2,1)}), bf16[32,200,128]{2,1,0:T(8,128)(2,1)S(1)}, u32[]{:S(2)}, u32[]{:S(2)}) %all-to-all-start.3) | async-done | bytes 1638432 | tf_op jit(solution)/shard_map/all_to_all | solution.py:16
  156.4 1.6 stack.43
  158.4 1.6 stack.42
  163.7 2.5 %collective-permute-start.13 = (bf16[2,160,288]{2,1,0:T(8,128)(2,1)S(1)}, bf16[2,160,288]{2,1,0:T(8,128)(2,1)}, u32[]{:S(2)}, u32[]{:S(2)}) collective-permute-start(bf16[2,160,288]{2,1,0:T(8,128)(2,1)S(1)} %get-tuple-element.22), channel_id=1, source_target_pairs={{0,2},{1,3},{2,0},{3,1},{4,6},{5,7},{6,4},{7,5},{8,10},{9,11},{10,... | collective-permute-start | bytes 552968 | tf_op jit(solution)/shard_map/ppermute | solution.py:29
  167.3 5.7 %all-to-all-start.4 = ((bf16[8,2,18,288]{3,1,2,0:T(2,128)(2,1)}), bf16[8,2,18,288]{3,1,2,0:T(2,128)(2,1)S(1)}, u32[]{:S(2)}, u32[]{:S(2)}) async-start(bf16[8,2,18,288]{3,1,2,0:T(2,128)(2,1)} %copy.53), calls=%async_computation.4 | async-start | bytes 442368 | tf_op jit(solution)/shard_map/all_to_all | solution.py:16
  173.0 4.8 %collective-permute-done.13 = bf16[2,160,288]{2,1,0:T(8,128)(2,1)} collective-permute-done((bf16[2,160,288]{2,1,0:T(8,128)(2,1)S(1)}, bf16[2,160,288]{2,1,0:T(8,128)(2,1)}, u32[]{:S(2)}, u32[]{:S(2)}) %collective-permute-start.13) | collective-permute-done | bytes 184352 | tf_op jit(solution)/shard_map/ppermute | solution.py:29
  179.9 4.0 %all-to-all-done.4 = bf16[8,2,18,288]{3,1,2,0:T(2,128)(2,1)S(1)} async-done(((bf16[8,2,18,288]{3,1,2,0:T(2,128)(2,1)}), bf16[8,2,18,288]{3,1,2,0:T(2,128)(2,1)S(1)}, u32[]{:S(2)}, u32[]{:S(2)}) %all-to-all-start.4) | async-done | bytes 165920 | tf_op jit(solution)/shard_map/all_to_all | solution.py:16
  (108 shorter events, 25.3 us)
Async XLA Ops:
  0.6 1.8 copy-start
  0.7 7.7 %copy-start.8 = (bf16[160,1152]{1,0:T(8,128)(2,1)S(1)}, bf16[160,1152]{1,0:T(8,128)(2,1)}, u32[]{:S(2)}) copy-start(bf16[160,1152]{1,0:T(8,128)(2,1)} %param.6) | copy-start | bytes 1105924
  2.4 6.2 %copy-start.9 = (bf16[160,1152]{1,0:T(8,128)(2,1)S(1)}, bf16[160,1152]{1,0:T(8,128)(2,1)}, u32[]{:S(2)}) copy-start(bf16[160,1152]{1,0:T(8,128)(2,1)} %param.7) | copy-start | bytes 1105924
  3.9 3.1 %copy-start.5 = (f32[160,288]{1,0:T(8,128)}, f32[160,288]{1,0:T(8,128)S(1)}, u32[]{:S(2)}) copy-start(f32[160,288]{1,0:T(8,128)S(1)} %fusion.69) | copy-start | bytes 552964
  4.7 12.6 %collective-permute-start.2 = (f32[2,40,288]{2,1,0:T(8,128)}, f32[2,40,288]{2,1,0:T(8,128)}, u32[]{:S(2)}, u32[]{:S(2)}) collective-permute-start(f32[2,40,288]{2,1,0:T(8,128)} %get-tuple-element.35), channel_id=1, source_target_pairs={{0,3},{1,2},{2,1},{3,0},{4,7},{5,6},{6,5},{7,4},{8,11},{9,10},{10,... | collective-permute-start | bytes 276488 | tf_op jit(solution)/shard_map/ppermute | solution.py:29
  6.3 11.0 %collective-permute-start = (f32[2,40,288]{2,1,0:T(8,128)}, f32[2,40,288]{2,1,0:T(8,128)}, u32[]{:S(2)}, u32[]{:S(2)}) collective-permute-start(f32[2,40,288]{2,1,0:T(8,128)} %get-tuple-element.36), channel_id=1, source_target_pairs={{0,1},{1,0},{2,3},{3,2},{4,5},{5,4},{6,7},{7,6},{8,9},{9,8},{10,11... | collective-permute-start | bytes 276488 | tf_op jit(solution)/shard_map/ppermute | solution.py:29
  7.0 10.4 %collective-permute-start.1 = (f32[2,40,288]{2,1,0:T(8,128)}, f32[2,40,288]{2,1,0:T(8,128)}, u32[]{:S(2)}, u32[]{:S(2)}) collective-permute-start(f32[2,40,288]{2,1,0:T(8,128)} %get-tuple-element.37), channel_id=1, source_target_pairs={{0,2},{1,3},{2,0},{3,1},{4,6},{5,7},{6,4},{7,5},{8,10},{9,11},{10,... | collective-permute-start | bytes 276488 | tf_op jit(solution)/shard_map/ppermute | solution.py:29
  9.8 7.6 %copy-start.6 = (f32[160,288]{1,0:T(8,128)S(1)}, f32[160,288]{1,0:T(8,128)}, u32[]{:S(2)}) copy-start(f32[160,288]{1,0:T(8,128)} %copy-done.5) | copy-start | bytes 552964
  11.4 19.5 %all-to-all-start = ((bf16[8,160,288]{2,1,0:T(8,128)(2,1)}), bf16[8,160,288]{2,1,0:T(8,128)(2,1)S(1)}, u32[]{:S(2)}, u32[]{:S(2)}) async-start(bf16[8,160,288]{2,1,0:T(8,128)(2,1)} %copy.46), calls=%async_computation | async-start | bytes 1966080 | tf_op jit(solution)/shard_map/all_to_all | solution.py:16
  19.9 12.3 %copy-start.7 = (bf16[2,40,1152]{2,1,0:T(8,128)(2,1)}, bf16[2,40,1152]{2,1,0:T(8,128)(2,1)S(1)}, u32[]{:S(2)}) copy-start(bf16[2,40,1152]{2,1,0:T(8,128)(2,1)S(1)} %multiply_convert_fusion) | copy-start | bytes 552964
  32.1 39.8 %all-to-all-start.1 = ((bf16[16,40,1152]{2,1,0:T(8,128)(2,1)}), bf16[16,40,1152]{2,1,0:T(8,128)(2,1)S(1)}, u32[]{:S(2)}, u32[]{:S(2)}) async-start(bf16[16,40,1152]{2,1,0:T(8,128)(2,1)} %broadcast_in_dim.31), calls=%async_computation.1 | async-start | bytes 2949120 | tf_op jit(solution)/shard_map/all_to_all | solution.py:16
  69.4 2.6 %collective-permute-start.3 = (bf16[320,1152]{1,0:T(8,128)(2,1)}, bf16[320,1152]{1,0:T(8,128)(2,1)}, u32[]{:S(2)}, u32[]{:S(2)}) collective-permute-start(bf16[320,1152]{1,0:T(8,128)(2,1)} %bitcast.14), channel_id=1, source_target_pairs={{0,1},{1,0},{2,3},{3,2},{4,5},{5,4},{6,7},{7,6},{8,9},{9,8},{10,11... | collective-permute-start | bytes 2211848 | tf_op jit(solution)/shard_map/ppermute | solution.py:20
  72.0 4.3 %copy-start.1 = (bf16[16,40,1152]{2,1,0:T(8,128)(2,1)}, bf16[16,40,1152]{2,1,0:T(8,128)(2,1)S(1)}, u32[]{:S(2)}) copy-start(bf16[16,40,1152]{2,1,0:T(8,128)(2,1)S(1)} %all-to-all-done.1) | copy-start | bytes 4423684
  76.2 15.8 %collective-permute-start.4 = (bf16[320,1152]{1,0:T(8,128)(2,1)}, bf16[320,1152]{1,0:T(8,128)(2,1)}, u32[]{:S(2)}, u32[]{:S(2)}) collective-permute-start(bf16[320,1152]{1,0:T(8,128)(2,1)} %convolution_convert_fusion), channel_id=1, source_target_pairs={{0,1},{1,0},{2,3},{3,2},{4,5},{5,4},{6,7},{7,6},{8,9},{9,8},{10,11... | collective-permute-start | bytes 2211848 | tf_op jit(solution)/shard_map/ppermute | solution.py:20
  78.3 0.8 copy-start.3
  84.6 35.4 %all-to-all-start.2 = ((bf16[16,40,1152]{2,1,0:T(8,128)(2,1)}), bf16[16,40,1152]{2,1,0:T(8,128)(2,1)}, u32[]{:S(2)}, u32[]{:S(2)}) async-start(bf16[16,40,1152]{2,1,0:T(8,128)(2,1)} %bitcast.16), calls=%async_computation.2 | async-start | bytes 2949120 | tf_op jit(solution)/shard_map/all_to_all | solution.py:16
  95.3 10.1 %collective-permute-start.5 = (bf16[40,1152]{1,0:T(8,128)(2,1)S(1)}, bf16[40,1152]{1,0:T(8,128)(2,1)S(1)}, u32[]{:S(2)}, u32[]{:S(2)}) collective-permute-start(bf16[40,1152]{1,0:T(8,128)(2,1)S(1)} %get-tuple-element.23), channel_id=1, source_target_pairs={{0,32},{32,64},{64,96},{96,128},{128,160},{160,192},{192,224},{224... | collective-permute-start | bytes 276488 | tf_op jit(solution)/shard_map/ppermute | solution.py:24
  96.3 9.8 %collective-permute-start.11 = (bf16[40,1152]{1,0:T(8,128)(2,1)S(1)}, bf16[40,1152]{1,0:T(8,128)(2,1)}, u32[]{:S(2)}, u32[]{:S(2)}) collective-permute-start(bf16[40,1152]{1,0:T(8,128)(2,1)S(1)} %get-tuple-element.24), channel_id=1, source_target_pairs={{0,224},{32,0},{64,32},{96,64},{128,96},{160,128},{192,160},{224,1... | collective-permute-start | bytes 276488 | tf_op jit(solution)/shard_map/ppermute | solution.py:24
  98.5 11.5 %collective-permute-start.10 = (bf16[40,1152]{1,0:T(8,128)(2,1)}, bf16[40,1152]{1,0:T(8,128)(2,1)S(1)}, u32[]{:S(2)}, u32[]{:S(2)}) collective-permute-start(bf16[40,1152]{1,0:T(8,128)(2,1)} %get-tuple-element.25), channel_id=1, source_target_pairs={{0,192},{32,224},{64,0},{96,32},{128,64},{160,96},{192,128},{224,1... | collective-permute-start | bytes 276488 | tf_op jit(solution)/shard_map/ppermute | solution.py:24
  98.9 11.1 %collective-permute-start.9 = (bf16[40,1152]{1,0:T(8,128)(2,1)}, bf16[40,1152]{1,0:T(8,128)(2,1)S(1)}, u32[]{:S(2)}, u32[]{:S(2)}) collective-permute-start(bf16[40,1152]{1,0:T(8,128)(2,1)} %get-tuple-element.26), channel_id=1, source_target_pairs={{0,160},{32,192},{64,224},{96,0},{128,32},{160,64},{192,96},{224,1... | collective-permute-start | bytes 276488 | tf_op jit(solution)/shard_map/ppermute | solution.py:24
  102.0 13.2 %collective-permute-start.8 = (bf16[40,1152]{1,0:T(8,128)(2,1)}, bf16[40,1152]{1,0:T(8,128)(2,1)}, u32[]{:S(2)}, u32[]{:S(2)}) collective-permute-start(bf16[40,1152]{1,0:T(8,128)(2,1)} %get-tuple-element.27), channel_id=1, source_target_pairs={{0,128},{32,160},{64,192},{96,224},{128,0},{160,32},{192,64},{224,... | collective-permute-start | bytes 276488 | tf_op jit(solution)/shard_map/ppermute | solution.py:24
  105.4 13.3 %collective-permute-start.7 = (bf16[40,1152]{1,0:T(8,128)(2,1)}, bf16[40,1152]{1,0:T(8,128)(2,1)}, u32[]{:S(2)}, u32[]{:S(2)}) collective-permute-start(bf16[40,1152]{1,0:T(8,128)(2,1)} %get-tuple-element.28), channel_id=1, source_target_pairs={{0,96},{32,128},{64,160},{96,192},{128,224},{160,0},{192,32},{224,... | collective-permute-start | bytes 276488 | tf_op jit(solution)/shard_map/ppermute | solution.py:24
  106.0 12.7 %collective-permute-start.6 = (bf16[40,1152]{1,0:T(8,128)(2,1)}, bf16[40,1152]{1,0:T(8,128)(2,1)}, u32[]{:S(2)}, u32[]{:S(2)}) collective-permute-start(bf16[40,1152]{1,0:T(8,128)(2,1)} %get-tuple-element.29), channel_id=1, source_target_pairs={{0,64},{32,96},{64,128},{96,160},{128,192},{160,224},{192,0},{224,... | collective-permute-start | bytes 276488 | tf_op jit(solution)/shard_map/ppermute | solution.py:24
  110.0 8.7 %copy-start.10 = (bf16[40,1152]{1,0:T(8,128)(2,1)}, bf16[40,1152]{1,0:T(8,128)(2,1)S(1)}, u32[]{:S(2)}) copy-start(bf16[40,1152]{1,0:T(8,128)(2,1)S(1)} %collective-permute-done.10) | copy-start | bytes 276484
  110.0 8.7 %copy-start.11 = (bf16[40,1152]{1,0:T(8,128)(2,1)}, bf16[40,1152]{1,0:T(8,128)(2,1)S(1)}, u32[]{:S(2)}) copy-start(bf16[40,1152]{1,0:T(8,128)(2,1)S(1)} %collective-permute-done.9) | copy-start | bytes 276484
  124.7 29.6 %all-to-all-start.3 = ((bf16[32,200,128]{2,1,0:T(8,128)(2,1)}), bf16[32,200,128]{2,1,0:T(8,128)(2,1)S(1)}, u32[]{:S(2)}, u32[]{:S(2)}) async-start(bf16[32,200,128]{2,1,0:T(8,128)(2,1)} %bitcast.129), calls=%async_computation.3 | async-start | bytes 3276800 | tf_op jit(solution)/shard_map/all_to_all | solution.py:16
  156.1 1.9 %copy-start.4 = (bf16[1152,288]{0,1:T(8,128)(2,1)S(1)}, bf16[1152,288]{0,1:T(8,128)(2,1)}, u32[]{:S(2)}) copy-start(bf16[1152,288]{0,1:T(8,128)(2,1)} %param.8) | copy-start | bytes 1990660
  160.0 1.5 copy-start.2
  162.5 10.5 %collective-permute-start.12 = (bf16[2,160,288]{2,1,0:T(8,128)(2,1)}, bf16[2,160,288]{2,1,0:T(8,128)(2,1)}, u32[]{:S(2)}, u32[]{:S(2)}) collective-permute-start(bf16[2,160,288]{2,1,0:T(8,128)(2,1)} %get-tuple-element.20), channel_id=1, source_target_pairs={{0,1},{1,0},{2,3},{3,2},{4,5},{5,4},{6,7},{7,6},{8,9},{9,8},{10,11... | collective-permute-start | bytes 552968 | tf_op jit(solution)/shard_map/ppermute | solution.py:29
  162.5 10.5 %collective-permute-start.14 = (bf16[2,160,288]{2,1,0:T(8,128)(2,1)}, bf16[2,160,288]{2,1,0:T(8,128)(2,1)}, u32[]{:S(2)}, u32[]{:S(2)}) collective-permute-start(bf16[2,160,288]{2,1,0:T(8,128)(2,1)} %get-tuple-element.21), channel_id=1, source_target_pairs={{0,3},{1,2},{2,1},{3,0},{4,7},{5,6},{6,5},{7,4},{8,11},{9,10},{10,... | collective-permute-start | bytes 552968 | tf_op jit(solution)/shard_map/ppermute | solution.py:29
  163.7 14.2 %collective-permute-start.13 = (bf16[2,160,288]{2,1,0:T(8,128)(2,1)S(1)}, bf16[2,160,288]{2,1,0:T(8,128)(2,1)}, u32[]{:S(2)}, u32[]{:S(2)}) collective-permute-start(bf16[2,160,288]{2,1,0:T(8,128)(2,1)S(1)} %get-tuple-element.22), channel_id=1, source_target_pairs={{0,2},{1,3},{2,0},{3,1},{4,6},{5,7},{6,4},{7,5},{8,10},{9,11},{10,... | collective-permute-start | bytes 552968 | tf_op jit(solution)/shard_map/ppermute | solution.py:29
  167.3 16.6 %all-to-all-start.4 = ((bf16[8,2,18,288]{3,1,2,0:T(2,128)(2,1)}), bf16[8,2,18,288]{3,1,2,0:T(2,128)(2,1)S(1)}, u32[]{:S(2)}, u32[]{:S(2)}) async-start(bf16[8,2,18,288]{3,1,2,0:T(2,128)(2,1)} %copy.53), calls=%async_computation.4 | async-start | bytes 442368 | tf_op jit(solution)/shard_map/all_to_all | solution.py:16
